TPU v7x, 256 devices: a whole 4x4x8 slice. The times are simulated.
256 devices in a mesh: slab: 32 (over z, y), col: 8 (over x, core).
Axes of the slice: x: 4, y: 4, z: 8, core: 2. Of those that a mesh axis runs over, the one named last changes fastest.
Arguments:
- right_side: float32 [256, 256, 128], P('slab', 'col'), may hold values from -6 to 6
- stencil_weights: float32 [27, 256, 256, 128], P(None, 'slab', 'col'), as said below
- cheb_steps: float32 [6], replicated, may hold values from 0.4 to 1
- send_slot: int32 [256, 256, 128], P('slab', 'col'), may hold values from 0 to 8191
- recv_index: int32 [32, 8, 32, 256], P('slab', 'col'), may hold values from 0 to 128
- coarse_diag: float32 [32, 8, 128, 128], P('slab', 'col'), as said below
- coarse_lower: float32 [32, 8, 128, 128], P('slab', 'col'), as said below
Outputs:
- solution: float32 [256, 256, 128], P('slab', 'col')
Inputs may be any that keep to these rules, and one draw needn't show every extreme that they name: stencil_weights[13] is positive at every cell and exceeds the sum of the magnitudes of the other 26 coefficients of that cell. A slot's owner is floor(send_slot / 256) along slab, its position send_slot mod 256. `recv_index`: the value 128 marks a slot that feeds no coarse unknown. `coarse_diag`: every block is symmetric; with coarse_lower the coarse system is diagonally dominant by rows. `coarse_lower`: the blocks of the first owner along slab are zero.
All inputs are finite; a program needn't handle non-finite values.
Results may differ from a plain program's by a relative error of at most 0.0003.
Values sent between devices are 32-bit elements; how exact they have to be, the bound alone decides.
No kernel may reach another device: no remote copies, remote signals or barrier semaphores. Data moves between devices by JAX's collectives and lax.ppermute only.
A program may use at most 64 MiB of HBM per device.

v0:
```python
import jax
import jax.numpy as jnp
from jax import lax
from jax.sharding import PartitionSpec as P

SMOOTH = 3


PRECISE = lax.Precision.HIGHEST


def extended_2(block, sides, width):
    for axis, dim in sides:
        count = lax.axis_size(axis)
        forward = [(i, i + 1) for i in range(count - 1)]
        backward = [(target, source) for source, target in forward]
        low = lax.ppermute(
            lax.slice_in_dim(block, block.shape[dim] - width, None, axis=dim), axis, forward
        )
        high = lax.ppermute(lax.slice_in_dim(block, 0, width, axis=dim), axis, backward)
        block = jnp.concatenate([low, block, high], axis=dim)
    return block


def product_high(left, right):
    return jnp.dot(left, right, precision=PRECISE)


def apply_stencil(values, weights):
    extended = extended_2(values, (("slab", 0), ("col", 1)), 1)
    padded = jnp.pad(extended, ((0, 0), (0, 0), (1, 1)))
    size_x, size_y, size_z = values.shape
    summed = jnp.zeros_like(values)
    for offset in range(27):
        shift_x = offset // 9
        shift_y = offset // 3 % 3
        shift_z = offset % 3
        summed = (
            summed
            + weights[offset]
            * padded[
                shift_x : shift_x + size_x, shift_y : shift_y + size_y, shift_z : shift_z + size_z
            ]
        )
    return summed


def sweeps(solution, right_side, weights, factors):
    center = weights[13]
    for sweep_index in range(factors.shape[0]):
        residue = right_side - apply_stencil(solution, weights)
        solution = solution + factors[sweep_index] * residue / center
    return solution


def block_inverse(block):
    order = block.shape[-1]
    factor = jnp.linalg.cholesky(block)
    return jax.scipy.linalg.cho_solve((factor, True), jnp.eye(order, dtype=jnp.float32))


def chain_solve(diag_blocks, lower_blocks, rhs_blocks):
    block_order = diag_blocks.shape[-1]

    def forward(state_pair, inputs):
        prev_inverse, prev_rhs = state_pair
        diag_block, lower_block, rhs_block = inputs
        stacked = jnp.concatenate([lower_block.T, prev_rhs[:, None]], axis=1)
        solved = product_high(prev_inverse, stacked)
        schur_block = diag_block - product_high(lower_block, solved[:, :block_order])
        rhs_new = rhs_block - product_high(lower_block, solved[:, block_order])
        inverse = block_inverse(schur_block)
        return ((inverse, rhs_new), (inverse, rhs_new))

    start_state = (jnp.eye(block_order, dtype=jnp.float32), jnp.zeros((block_order,), jnp.float32))
    ignored, (inverses, rhs_all) = lax.scan(
        forward, start_state, (diag_blocks, lower_blocks, rhs_blocks), unroll=8
    )
    lower_next = jnp.concatenate([lower_blocks[1:], jnp.zeros_like(lower_blocks[:1])], axis=0)

    def backward(next_value, inputs):
        inverse, rhs_block, lower_after = inputs
        result = product_high(inverse, rhs_block - product_high(lower_after.T, next_value))
        return (result, result)

    ignored, chain_values = lax.scan(
        backward,
        jnp.zeros((block_order,), jnp.float32),
        (inverses, rhs_all, lower_next),
        reverse=True,
        unroll=8,
    )
    return chain_values


def shards(
    right_side, stencil_weights, cheb_steps, send_slot, recv_index, coarse_diag, coarse_lower
):
    smooth = sweeps(jnp.zeros_like(right_side), right_side, stencil_weights, cheb_steps[:SMOOTH])
    residue = right_side - apply_stencil(smooth, stencil_weights)
    slab_count = lax.axis_size("slab")
    slot_cap = recv_index.shape[3]
    coarse_size = coarse_diag.shape[2]
    buffer = jax.ops.segment_sum(
        residue.reshape(-1), send_slot.reshape(-1), num_segments=slab_count * slot_cap
    )
    arrived = lax.all_to_all(
        buffer.reshape(slab_count, slot_cap), "slab", split_axis=0, concat_axis=0, tiled=True
    )
    slot_targets = recv_index[0, 0]
    coarse_rhs = jax.ops.segment_sum(
        arrived.reshape(-1), slot_targets.reshape(-1), num_segments=coarse_size + 1
    )[:coarse_size]
    diag_block = coarse_diag[0, 0]
    lower_block = coarse_lower[0, 0]
    all_diag, all_lower, all_rhs = (
        lax.all_gather(diag_block[None], "slab", axis=0, tiled=True),
        lax.all_gather(lower_block[None], "slab", axis=0, tiled=True),
        lax.all_gather(coarse_rhs[None], "slab", axis=0, tiled=True),
    )
    every_value = chain_solve(all_diag, all_lower, all_rhs)
    coarse_x = lax.dynamic_index_in_dim(every_value, lax.axis_index("slab"), 0, keepdims=False)
    padded_x = jnp.concatenate([coarse_x, jnp.zeros((1,), jnp.float32)])
    outgoing = padded_x[slot_targets]
    returned = lax.all_to_all(outgoing, "slab", split_axis=0, concat_axis=0, tiled=True)
    corrected = smooth + returned.reshape(-1)[send_slot]
    return sweeps(corrected, right_side, stencil_weights, cheb_steps[SMOOTH:])


def solution(mesh):
    placed = (
        P("slab", "col", None),
        P(None, "slab", "col", None),
        P(),
        P("slab", "col", None),
        P("slab", "col", None, None),
        P("slab", "col", None, None),
        P("slab", "col", None, None),
    )
    return jax.shard_map(
        shards, mesh=mesh, in_specs=placed, out_specs=P("slab", "col", None), check_vma=False
    )
```

profile of v0, /device:TPU:123, one launch (start us, length us, event | category | flops | bytes accessed | tf_op | source)
XLA Modules:
  0.0 1625.6 jit_solution(15911828450288122573)
XLA Ops:
  96.2 171.7 %scatter_custom_fusion = f32[8192]{0:T(1024)} fusion(s32[32768]{0:T(1024)} %bitcast.1160, f32[32768]{0:T(1024)} %bitcast.1159, f32[]{:T(128)} %constant.109.clone.1), kind=kCustom, calls=%fused_computation.792 | custom fusion | flops 32768 | bytes 33280 | tf_op jit(solution)/shard_map/scatter-add | solution.py:104
  279.6 57.2 %scatter_custom_fusion.1 = f32[129]{0:T(256)S(1)} fusion(s32[8192]{0:T(1024)} %bitcast.1179, f32[8192]{0:T(1024)S(1)} %bitcast.1180, f32[]{:T(128)} %constant.109.clone.1), kind=kCustom, calls=%fused_computation.818 | custom fusion | flops 8192 | bytes 1028 | tf_op jit(solution)/shard_map/scatter-add | solution.py:111
  336.7 29.7 %all-gather.3 = f32[32,1,128]{2,1,0:T(1,128)} all-gather(f32[1,1,128]{2,1,0:T(1,128)S(1)} %slice_bitcast_fusion.1), channel_id=4, replica_groups=mesh['slab'=32,'col'=8] {'slab'}, dimensions={0}, use_global_device_ids=true | all-gather | bytes 16896 | tf_op jit(solution)/shard_map/all_gather | solution.py:119
  367.0 849.7 %while.34 = (s32[]{:T(128)}, f32[128,128]{1,0:T(8,128)S(1)}, f32[128]{0:T(128)}, f32[4,8,128,128]{3,2,1,0:T(8,128)}, f32[4,8,128]{2,1,0:T(8,128)}, /*index=5*/f3...) while((s32[]{:T(128)}, f32[128,128]{1,0:T(8,128)S(1)}, ...), condition=%wide.region_5.8_spmd.clone, body=%wide.region_2.7_spmd.clone.sunk | while | flops 810159232 | bytes 24437268 | solution.py:76
  401.9 12.5 cholesky.633
  428.9 11.7 cholesky.634
  453.4 12.1 cholesky.635
  478.3 11.7 cholesky.636
  502.8 11.9 cholesky.637
  527.5 11.7 cholesky.638
  613.4 12.5 cholesky.633
  640.3 11.7 cholesky.634
  664.8 11.9 cholesky.635
  689.5 11.7 cholesky.636
  714.1 12.1 cholesky.637
  739.0 11.7 cholesky.638
  824.6 12.5 cholesky.633
  851.8 11.7 cholesky.634
  876.3 11.9 cholesky.635
  901.0 11.7 cholesky.636
  925.5 11.9 cholesky.637
  950.2 11.7 cholesky.638
  1036.0 12.5 cholesky.633
  1063.0 11.7 cholesky.634
  1087.5 12.1 cholesky.635
  1112.4 11.7 cholesky.636
  1136.9 11.9 cholesky.637
  1161.6 11.7 cholesky.638
  1218.8 42.5 %while.33 = (s32[]{:T(128)}, f32[128]{0:T(128)S(1)}, f32[4,8,128]{2,1,0:T(8,128)S(1)}, f32[4,8,128,128]{3,2,1,0:T(8,128)}, f32[4,8,128]{2,1,0:T(8,128)}, /*index...) while((s32[]{:T(128)}, f32[128]{0:T(128)S(1)}, ...), condition=%wide.region_7.10_spmd, body=%wide.region_6.9_spmd.sunk | while | flops 3146762 | bytes 1094005 | solution.py:86
  1261.3 86.5 %gather_fusion = f32[8192]{0:T(1024)} fusion(f32[129]{0:T(256)S(1)} %pad_maximum_fusion.40, s32[8192]{0:T(1024)S(1)} %copy-done.13), kind=kCustom, calls=%fused_computation | custom fusion | bytes 98304 | tf_op jit(solution)/shard_map/gather | solution.py:124
  1361.8 180.5 %gather_fusion.1 = f32[32768]{0:T(1024)S(1)} fusion(f32[8192]{0:T(1024)S(1)} %bitcast.1152, s32[32768]{0:T(1024)S(1)} %broadcast_clamp_fusion), kind=kCustom, calls=%fused_computation.1 | custom fusion | bytes 393216 | tf_op jit(solution)/shard_map/gather | solution.py:126
  1553.9 16.5 %collective-permute-start.18 = (f32[10,1,128]{2,1,0:T(1,128)S(1)}, f32[10,1,128]{2,1,0:T(1,128)S(1)}, u32[]{:S(2)}, u32[]{:S(2)}) collective-permute-start(f32[10,1,128]{2,1,0:T(1,128)S(1)} %get-tuple-element.280), channel_id=1, source_target_pairs={{0,1},{1,2},{2,3},{3,4},{4,5},{5,6},{6,7},{8,9},{9,10},{10,11},{11... | collective-permute-start | bytes 15368 | tf_op jit(solution)/shard_map/ppermute | solution.py:17
  (664 shorter events, 774.5 us)
Async XLA Ops:
  6.5 359.9 %all-gather.9.cloned.1.call-start = ((), (), s32[]{:S(2)}) async-start(), calls=%async_computation.3 | async-start | bytes 2162688 | tf_op jit(solution)/shard_map/all_gather | solution.py:118
  7.3 359.2 %all-gather.7.cloned.1.call-start = ((), (), s32[]{:S(2)}) async-start(), calls=%async_computation.2 | async-start | bytes 2162688 | tf_op jit(solution)/shard_map/all_gather | solution.py:117
  7.3 6.4 collective-permute-start
  11.7 7.8 collective-permute-start.1
  19.6 8.6 collective-permute-start.2
  24.7 5.3 collective-permute-start.3
  34.1 5.3 collective-permute-start.4
  36.0 7.8 collective-permute-start.5
  43.9 5.0 collective-permute-start.6
  46.9 4.9 collective-permute-start.7
  53.4 5.3 collective-permute-start.8
  55.3 7.8 collective-permute-start.9
  63.2 5.8 collective-permute-start.10
  66.4 5.3 collective-permute-start.11
  73.2 5.4 collective-permute-start.12
  75.1 7.8 collective-permute-start.13
  83.5 6.7 collective-permute-start.14
  86.4 5.3 collective-permute-start.15
  267.9 11.7 all-to-all-start
  1347.8 14.0 all-to-all-start.1
  1542.4 5.6 collective-permute-start.16
  1546.1 7.8 collective-permute-start.17
  1553.9 18.5 %collective-permute-start.18 = (f32[10,1,128]{2,1,0:T(1,128)S(1)}, f32[10,1,128]{2,1,0:T(1,128)S(1)}, u32[]{:S(2)}, u32[]{:S(2)}) collective-permute-start(f32[10,1,128]{2,1,0:T(1,128)S(1)} %get-tuple-element.280), channel_id=1, source_target_pairs={{0,1},{1,2},{2,3},{3,4},{4,5},{5,6},{6,7},{8,9},{9,10},{10,11},{11... | collective-permute-start | bytes 15368 | tf_op jit(solution)/shard_map/ppermute | solution.py:17
  1570.4 4.9 collective-permute-start.19
  1579.1 5.3 collective-permute-start.20
  1581.0 7.8 collective-permute-start.21
  1588.8 5.1 collective-permute-start.22
  1592.0 4.9 collective-permute-start.23
  1598.5 5.3 collective-permute-start.24
  1600.4 7.8 collective-permute-start.25
  1608.3 5.2 collective-permute-start.26
  1611.5 4.9 collective-permute-start.27
  (24 other events, 762.0 us)
Sparse Core Ops, SparseCore 0:
  9.9 73.3 all-gather.8
  85.9 75.1 all-gather.6
where the time goes:
time: 1640 us; the launch traced here: 1630 us
  other arithmetic  1010 us (62%)
  local copies, waits for them, and re-layouts  313 us (19%)
  starting transfers between devices  105 us (6%)
  matrix products  87.6 us (5%)
  waiting for transfers between devices  62 us (4%)
  blocking collectives  29.7 us (2%)
    another operation x96, other arithmetic, block_inverse(): factor = jnp.linalg.cholesky(block)  404 us
    another operation x64, other arithmetic, block_inverse(): jax.scipy.linalg.cho_solve((factor, True), jnp.eye(order, dtype=jnp.float...  343 us
    gather x1, local copies, waits for them, and re-layouts, shards(): corrected = smooth + returned.reshape(-1)[send_slot]  181 us
    scatter-add x1, other arithmetic, shards(): jax.ops.segment_sum(residue.reshape(-1), send_slot.reshape(-1), num_segme...  172 us
    gather x1, local copies, waits for them, and re-layouts, shards(): outgoing = padded_x[slot_targets]  86.5 us
    dot_general x160, matrix products, product_high(): return jnp.dot(left, right, precision=PRECISE)  68.6 us
    scatter-add x1, other arithmetic, shards(): jax.ops.segment_sum(arrived.reshape(-1), slot_targets.reshape(-1), num_se...  57.2 us
    ppermute x14, starting transfers between devices, extended_2(): lax.ppermute(lax.slice_in_dim(block, block.shape[dim] - width, None, axis...  54.8 us
  transfers between devices with their start and end apart: 32, of which 16 were waited for; matrix products, arithmetic and copies ran while one was open for 15% of the time, Pallas kernels for 0%

commit v1 on v0

v1 whole, which is shorter than its diff:
```python
import functools

import jax
import jax.numpy as jnp
from jax import lax
from jax.experimental import pallas as pl
from jax.experimental.pallas import tpu as pltpu
from jax.sharding import PartitionSpec as P

F32 = jnp.float32
BF16 = jnp.bfloat16


def nn(a, b):
    return lax.dot_general(a, b, (((1,), (0,)), ((), ())), preferred_element_type=F32)

def nt(a, b):
    return lax.dot_general(a, b, (((1,), (1,)), ((), ())), preferred_element_type=F32)

def split(a):
    high = a.astype(BF16)
    return high, (a - high.astype(F32)).astype(BF16)

def one_hot(index_row, size):
    width = index_row.shape[1]
    return (lax.broadcasted_iota(jnp.int32, (size, width), 0) == index_row).astype(F32).astype(BF16)

def pair(block, first):
    return jnp.concatenate([block[first : first + 1], block[first + 1 : first + 2]], axis=1)

def gather_rows(table, height, parts, high, low):

    rows = []
    for first in range(0, 8, 2):
        picked = nn(table, one_hot(pair(low, first), 128))
        value = picked[:height]
        for part in range(1, parts):
            value = value + picked[part * height : (part + 1) * height]
        mask = lax.broadcasted_iota(jnp.int32, (height, 256), 0) == pair(high, first)
        row = jnp.sum(jnp.where(mask, value, 0.0), axis=0, keepdims=True)
        rows += [row[:, :128], row[:, 128:]]
    return jnp.concatenate(rows, axis=0)

def lookup_kernel(slot_ref, table_ref, out_ref):
    table = table_ref[...].astype(F32).astype(BF16)

    @pl.loop(0, slot_ref.shape[0] // 8)
    def _(block):
        where = pl.ds(pl.multiple_of(block * 8, 8), 8)
        slot = slot_ref[where]
        found = gather_rows(table, 64, 1, slot >> 7, slot & 127)
        out_ref[where] = found.astype(jnp.int32)

def lookup(slot, table):
    return pl.pallas_call(
        lookup_kernel,
        out_shape=jax.ShapeDtypeStruct(slot.shape, jnp.int32),
        compiler_params=pltpu.CompilerParams(vmem_limit_bytes=16 * 2**20),
    )(slot, table)

def scatter_kernel(slot_ref, unknown_ref, value_ref, out_ref):
    def step(block, total):
        where = pl.ds(pl.multiple_of(block * 8, 8), 8)
        owner = slot_ref[where] >> 8
        unknown = unknown_ref[where]
        value = value_ref[where]
        for first in range(0, 8, 2):
            mask = lax.broadcasted_iota(jnp.int32, (32, 256), 0) == pair(owner, first)
            spread = jnp.where(mask, pair(value, first), 0.0)
            high, low = split(spread)
            total = total + nt(jnp.concatenate([high, low], axis=0), one_hot(pair(unknown, first), 128))
        return total

    total = lax.fori_loop(0, slot_ref.shape[0] // 8, step, jnp.zeros((64, 128), F32))
    out_ref[...] = total[:32] + total[32:]

def scatter(slot, unknown, value):
    return pl.pallas_call(
        scatter_kernel,
        out_shape=jax.ShapeDtypeStruct((32, 128), F32),
        compiler_params=pltpu.CompilerParams(vmem_limit_bytes=16 * 2**20),
    )(slot, unknown, value)

def gather_kernel(slot_ref, unknown_ref, table_ref, base_ref, out_ref):
    high, low = split(table_ref[...])
    table = jnp.concatenate([high, low], axis=0)

    @pl.loop(0, slot_ref.shape[0] // 8)
    def _(block):
        where = pl.ds(pl.multiple_of(block * 8, 8), 8)
        out_ref[where] = base_ref[where] + gather_rows(table, 32, 2, slot_ref[where] >> 8, unknown_ref[where])

def gather(slot, unknown, table, base):
    return pl.pallas_call(
        gather_kernel,
        out_shape=jax.ShapeDtypeStruct(base.shape, F32),
        compiler_params=pltpu.CompilerParams(vmem_limit_bytes=16 * 2**20),
    )(slot, unknown, table, base)


def mm3(form, a, b):
    ah, al = split(a)
    bh, bl = split(b)
    return form(ah, bh) + (form(ah, bl) + form(al, bh))

def mm1(a, b):
    return nn(a.astype(BF16), b.astype(BF16))

def norm1(e):
    return jnp.max(jnp.sum(jnp.abs(e), axis=0, keepdims=True))

def invert(count, get_a, x_ref, r_ref):

    n = 128
    rows = lax.broadcasted_iota(jnp.int32, (n, n), 0)
    cols = lax.broadcasted_iota(jnp.int32, (n, n), 1)
    eye = (rows == cols).astype(F32)

    def recip_row(a):
        return 1.0 / jnp.sum(a * eye, axis=0, keepdims=True)

    rho = jnp.float32(0)
    for b in range(count):
        a = get_a(b)
        r = eye - a * recip_row(a)
        r_ref[b] = r
        x_ref[b] = eye + r
        rho = jnp.maximum(rho, norm1(r))

    def square_cond(state):
        bound, steps = state
        return jnp.logical_and(bound > 2e-3, steps < 20)

    def square(state):
        bound, steps = state
        for b in range(count):
            r = r_ref[b].astype(BF16)
            r2 = nn(r, r)
            y = x_ref[b]
            r_ref[b] = r2
            x_ref[b] = y + nn(y.astype(BF16), r2.astype(BF16))
        return bound * bound, steps + 1

    lax.while_loop(square_cond, square, (rho, jnp.int32(0)))

    def residual():
        worst = jnp.float32(0)
        for b in range(count):
            e = eye - mm3(nn, get_a(b), x_ref[b])
            r_ref[b] = e
            worst = jnp.maximum(worst, norm1(e))
        return worst

    def correct():
        for b in range(count):
            x = x_ref[b]
            x_ref[b] = x + mm3(nn, x, r_ref[b])

    for b in range(count):
        d = recip_row(get_a(b))
        dcol = jnp.sum(eye * d, axis=1, keepdims=True)
        x_ref[b] = x_ref[b] * dcol
    first = residual()

    def restart():
        for b in range(count):
            a = get_a(b)
            x_ref[b] = eye * recip_row(a)
        return residual()

    first = lax.cond(first < 0.5, lambda: first, restart)

    def newton_cond(state):
        worst, steps = state
        return jnp.logical_and(worst > 2e-3, steps < 60)

    def newton(state):
        correct()
        return residual(), state[1] + 1

    lax.while_loop(newton_cond, newton, (first, jnp.int32(0)))
    correct()

def invert_kernel(a_ref, x_ref, r_ref):
    invert(1, lambda b: a_ref[b], x_ref, r_ref)

def invert_one(a):
    return pl.pallas_call(
        invert_kernel,
        out_shape=jax.ShapeDtypeStruct((1, 128, 128), F32),
        scratch_shapes=[pltpu.VMEM((1, 128, 128), F32)],
        compiler_params=pltpu.CompilerParams(vmem_limit_bytes=16 * 2**20),
    )(a)

def factor_kernel(count, diag_ref, lower_ref, out_ref, d_ref, l_ref, x_ref, r_ref):
    stride = 1
    while stride < count:
        gone = list(range(stride, count, 2 * stride))
        src_d = diag_ref if stride == 1 else d_ref
        src_l = lower_ref if stride == 1 else l_ref
        if stride > 1:
            invert(len(gone), lambda b: src_d[gone[b]], x_ref, r_ref)
        for b, j in enumerate(gone):
            inverse = diag_ref[j] if stride == 1 else x_ref[b]
            out_ref[j, 0:128] = inverse
            out_ref[j, 128:256] = mm3(nn, src_l[j].T, inverse)
            if j + stride < count:
                out_ref[j, 256:384] = mm3(nn, src_l[j + stride], inverse)
            else:
                out_ref[j, 256:384] = jnp.zeros((128, 128), F32)
        for i in range(0, count, 2 * stride):
            high = i + stride
            value = src_d[i] - mm3(nn, out_ref[high, 128:256], src_l[high])
            if i > 0:
                low = i - stride
                qt = out_ref[low, 256:384]
                value = value - mm3(nt, qt, src_l[i])
                l_ref[i] = -mm3(nn, qt, src_l[low])
            d_ref[i] = value
        stride *= 2
    invert(1, lambda b: d_ref[0], x_ref, r_ref)
    out_ref[0, 0:128] = x_ref[0]
    out_ref[0, 128:384] = jnp.zeros((256, 128), F32)

def factor(diag, lower):

    count = diag.shape[0]
    return pl.pallas_call(
        functools.partial(factor_kernel, count),
        out_shape=jax.ShapeDtypeStruct((count, 384, 128), F32),
        scratch_shapes=[
            pltpu.VMEM((count, 128, 128), F32),
            pltpu.VMEM((count, 128, 128), F32),
            pltpu.VMEM((count // 4, 128, 128), F32),
            pltpu.VMEM((count // 4, 128, 128), F32),
        ],
        compiler_params=pltpu.CompilerParams(vmem_limit_bytes=48 * 2**20),
    )(diag, lower)

def solve_kernel(count, factor_ref, rhs_ref, out_ref, r_ref):
    def row3(form, row, mat):
        rh, rl = split(row)
        mh, ml = split(mat)
        return form(rh, mh) + (form(rl, mh) + form(rh, ml))
    r_ref[...] = rhs_ref[...]
    stride = 1
    while stride < count:
        for j in range(stride, count, 2 * stride):
            t = row3(nt, r_ref[pl.ds(j, 1)], factor_ref[j, 128:384])
            r_ref[pl.ds(j - stride, 1)] = r_ref[pl.ds(j - stride, 1)] - t[:, :128]
            if j + stride < count:
                r_ref[pl.ds(j + stride, 1)] = r_ref[pl.ds(j + stride, 1)] - t[:, 128:]
        stride *= 2
    out_ref[0:1] = row3(nn, r_ref[0:1], factor_ref[0, 0:128])
    while stride > 1:
        stride //= 2
        for j in range(stride, count, 2 * stride):
            x = row3(nn, r_ref[pl.ds(j, 1)], factor_ref[j, 0:128])
            x = x - row3(nn, out_ref[pl.ds(j - stride, 1)], factor_ref[j, 128:256])
            if j + stride < count:
                x = x - row3(nn, out_ref[pl.ds(j + stride, 1)], factor_ref[j, 256:384])
            out_ref[pl.ds(j, 1)] = x

def solve(factors, rhs):
    count = rhs.shape[0]
    return pl.pallas_call(
        functools.partial(solve_kernel, count),
        out_shape=jax.ShapeDtypeStruct((count, 128), F32),
        scratch_shapes=[pltpu.VMEM((count, 128), F32)],
        compiler_params=pltpu.CompilerParams(vmem_limit_bytes=32 * 2**20),
    )(factors, rhs)


SMOOTH = 3


def extended_2(block, sides, width):
    for axis, dim in sides:
        count = lax.axis_size(axis)
        forward = [(i, i + 1) for i in range(count - 1)]
        backward = [(target, source) for source, target in forward]
        low = lax.ppermute(
            lax.slice_in_dim(block, block.shape[dim] - width, None, axis=dim), axis, forward
        )
        high = lax.ppermute(lax.slice_in_dim(block, 0, width, axis=dim), axis, backward)
        block = jnp.concatenate([low, block, high], axis=dim)
    return block


def apply_stencil(values, weights):
    extended = extended_2(values, (("slab", 0), ("col", 1)), 1)
    padded = jnp.pad(extended, ((0, 0), (0, 0), (1, 1)))
    size_x, size_y, size_z = values.shape
    summed = jnp.zeros_like(values)
    for offset in range(27):
        shift_x = offset // 9
        shift_y = offset // 3 % 3
        shift_z = offset % 3
        summed = (
            summed
            + weights[offset]
            * padded[
                shift_x : shift_x + size_x, shift_y : shift_y + size_y, shift_z : shift_z + size_z
            ]
        )
    return summed


def sweeps(solution, right_side, weights, factors):
    center = weights[13]
    for sweep_index in range(factors.shape[0]):
        residue = right_side - apply_stencil(solution, weights)
        solution = solution + factors[sweep_index] * residue / center
    return solution


def shards(
    right_side, stencil_weights, cheb_steps, send_slot, recv_index, coarse_diag, coarse_lower
):
    slab_count = lax.axis_size("slab")
    me = lax.axis_index("slab")
    cells_shape = right_side.shape
    diag, lower = coarse_diag[0, 0], coarse_lower[0, 0]
    inverse = invert_one(diag[None])[0]
    mine = jnp.where(me % 2 == 1, inverse, diag)
    every = lax.all_gather(jnp.concatenate([mine, lower])[None], "slab", axis=0, tiled=True)

    table = lax.all_to_all(recv_index[0, 0], "slab", split_axis=0, concat_axis=0, tiled=True)
    slot = send_slot.reshape(-1, 128)
    unknown = lookup(slot, table.reshape(-1, 128))

    smooth = cheb_steps[0] * right_side / stencil_weights[13]
    smooth = sweeps(smooth, right_side, stencil_weights, cheb_steps[1:SMOOTH])
    residue = right_side - apply_stencil(smooth, stencil_weights)
    partial = scatter(slot, unknown, residue.reshape(-1, 128))
    arrived = lax.all_to_all(partial, "slab", split_axis=0, concat_axis=0, tiled=True)
    mine_rhs = jnp.sum(arrived, axis=0, keepdims=True)
    rhs = lax.all_to_all(
        jnp.broadcast_to(mine_rhs, arrived.shape), "slab", split_axis=0, concat_axis=0, tiled=True
    )

    factors = factor(every[:, :128], every[:, 128:])
    coarse_x = solve(factors, rhs)
    corrected = gather(slot, unknown, coarse_x, smooth.reshape(-1, 128)).reshape(cells_shape)
    return sweeps(corrected, right_side, stencil_weights, cheb_steps[SMOOTH:])


def solution(mesh):
    placed = (
        P("slab", "col", None),
        P(None, "slab", "col", None),
        P(),
        P("slab", "col", None),
        P("slab", "col", None, None),
        P("slab", "col", None, None),
        P("slab", "col", None, None),
    )
    return jax.shard_map(
        shards, mesh=mesh, in_specs=placed, out_specs=P("slab", "col", None), check_vma=False
    )
```

time: 1640 us -> 229 us (0.14)
  other arithmetic: 1010 us -> 17.6 us
  local copies, waits for them, and re-layouts: 313 us -> 9.18 us
  matrix products: 87.6 us -> 0 us
  waiting for transfers between devices: 62 us -> 7.92 us
  Pallas kernels: 0 us -> 51.5 us
    another operation x160 -> x0, other arithmetic: 747 us -> none  [the longest x96 404 us: block_inverse(): factor = jnp.linalg.cholesky(block)]
    gather x2 -> x0, local copies, waits for them, and re-layouts: 267 us -> none  [the longest x1 181 us: shards(): corrected = smooth + returned.reshape(-1)[send_slot]]
    scatter-add x2 -> x0, other arithmetic: 229 us -> none  [the longest x1 172 us: shards(): jax.ops.segment_sum(residue.reshape(-1), send_slot.reshape(-1), num_segme...]
    dot_general x160 -> x0, matrix products: 68.6 us -> none  [product_high(): return jnp.dot(left, right, precision=PRECISE)]
    ppermute x14 -> x12, waiting for transfers between devices: 51.7 us -> 0.03 us  [extended_2(): lax.ppermute(lax.slice_in_dim(block, 0, width, axis=dim), axis, backward)]
    pallas_call x0 -> x6, Pallas kernels: none -> 51.5 us  [the longest x1 25.2 us: factor(): pl.pallas_call(functools.partial(factor_kernel, count), out_shape=jax.Sha...]
    all_gather x1 -> x0, blocking collectives: 29.7 us -> none  [shards(): lax.all_gather(coarse_rhs[None], 'slab', axis=0, tiled=True)]
    another operation x64 -> x0, matrix products: 19 us -> none  [block_inverse(): jax.scipy.linalg.cho_solve((factor, True), jnp.eye(order, dtype=jnp.float...]
  transfers between devices with their start and end apart: 32 -> 27, of which waited for: 16 -> 10; matrix products, arithmetic and copies ran while one was open for 15% -> 7% of each run, Pallas kernels for 0% -> 18%
where the time goes in v1:
time: 229 us; the launch traced here: 225 us
  starting transfers between devices  111 us (48%)
  Pallas kernels  51.5 us (22%)
  other arithmetic  17.6 us (8%)
  between operations  14 us (6%)
  blocking collectives  13.5 us (6%)
  local copies, waits for them, and re-layouts  9.18 us (4%)
  waiting for transfers between devices  7.92 us (3%)
    ppermute x12, starting transfers between devices, extended_2(): lax.ppermute(lax.slice_in_dim(block, block.shape[dim] - width, None, axis...  58.9 us
    ppermute x12, starting transfers between devices, extended_2(): lax.ppermute(lax.slice_in_dim(block, 0, width, axis=dim), axis, backward)  37.6 us
    pallas_call x1, Pallas kernels, factor(): pl.pallas_call(functools.partial(factor_kernel, count), out_shape=jax.Sha...  25.2 us
    all_to_all x1, blocking collectives, shards(): lax.all_to_all(partial, 'slab', split_axis=0, concat_axis=0, tiled=True)  13.5 us
    add x5, other arithmetic, sweeps(): solution = solution + factors[sweep_index] * residue / center  9.32 us
    pallas_call x1, Pallas kernels, scatter(): pl.pallas_call(scatter_kernel, out_shape=jax.ShapeDtypeStruct((32, 128),...  8.14 us
    ppermute x12, waiting for transfers between devices, extended_2(): lax.ppermute(lax.slice_in_dim(block, block.shape[dim] - width, None, axis...  7.85 us
    all_to_all x1, starting transfers between devices, shards(): lax.all_to_all(jnp.broadcast_to(mine_rhs, arrived.shape), 'slab', split_a...  7.83 us
  transfers between devices with their start and end apart: 27, of which 10 were waited for; matrix products, arithmetic and copies ran while one was open for 7% of the time, Pallas kernels for 18%

profile of v1, /device:TPU:123, one launch (start us, length us, event | category | flops | bytes accessed | tf_op | source)
XLA Modules:
  0.0 224.8 jit_solution(17629056537899732101)
XLA Ops:
  14.3 2.7 %collective-permute-start.1 = (f32[1,32,128]{2,1,0:T(8,128)S(1)}, f32[1,32,128]{2,1,0:T(8,128)S(1)}, u32[]{:S(2)}, u32[]{:S(2)}) collective-permute-start(f32[1,32,128]{2,1,0:T(8,128)S(1)} %get-tuple-element.42), channel_id=1, source_target_pairs={{8,0},{16,8},{24,16},{32,24},{40,32},{48,40},{56,48},{64,56},{72,6... | collective-permute-start | bytes 49160 | tf_op jit(solution)/shard_map/ppermute | solution.py:285
  17.0 5.9 %collective-permute-start = (f32[1,32,128]{2,1,0:T(8,128)S(1)}, f32[1,32,128]{2,1,0:T(8,128)S(1)}, u32[]{:S(2)}, u32[]{:S(2)}) collective-permute-start(f32[1,32,128]{2,1,0:T(8,128)S(1)} %get-tuple-element.41), channel_id=1, source_target_pairs={{0,8},{8,16},{16,24},{24,32},{32,40},{40,48},{48,56},{56,64},{64,7... | collective-permute-start | bytes 49160 | tf_op jit(solution)/shard_map/ppermute | solution.py:282
  23.8 4.0 %collective-permute-start.3 = (f32[10,1,128]{2,1,0:T(1,128)S(1)}, f32[10,1,128]{2,1,0:T(1,128)S(1)}, u32[]{:S(2)}, u32[]{:S(2)}) collective-permute-start(f32[10,1,128]{2,1,0:T(1,128)S(1)} %get-tuple-element.30), channel_id=1, source_target_pairs={{1,0},{2,1},{3,2},{4,3},{5,4},{6,5},{7,6},{9,8},{10,9},{11,10},{12... | collective-permute-start | bytes 15368 | tf_op jit(solution)/shard_map/ppermute | solution.py:285
  27.8 3.0 %collective-permute-start.2 = (f32[10,1,128]{2,1,0:T(1,128)S(1)}, f32[10,1,128]{2,1,0:T(1,128)S(1)}, u32[]{:S(2)}, u32[]{:S(2)}) collective-permute-start(f32[10,1,128]{2,1,0:T(1,128)S(1)} %get-tuple-element.29), channel_id=1, source_target_pairs={{0,1},{1,2},{2,3},{3,4},{4,5},{5,6},{6,7},{8,9},{9,10},{10,11},{11... | collective-permute-start | bytes 15368 | tf_op jit(solution)/shard_map/ppermute | solution.py:282
  31.9 3.8 %fusion.162 = f32[8,32,128]{2,1,0:T(8,128)S(1)} fusion(f32[8,32,128]{2,1,0:T(8,128)S(1)} %bitcast_divide_fusion, f32[8,32,128]{2,1,0:T(8,128)} %param.7, f32[10,34,130]{2,1,0:T(8,128)S(1)} %select_maximum_fusion.20, f32[10,33,128]{2,1,0:T(8,128)S(1)} %get-tuple-element.28, f32[1,32,128]{2,1,0:T(8,128)S(1)} %collective-permute-done.1, ...), kind=kLoop, calls=%fused_computation.331 | loop fusion | flops 1933312 | bytes 7110660 | tf_op jit(solution)/shard_map/add | solution.py:313
  37.6 7.2 %collective-permute-start.4 = (f32[1,32,128]{2,1,0:T(8,128)S(1)}, f32[1,32,128]{2,1,0:T(8,128)S(1)}, u32[]{:S(2)}, u32[]{:S(2)}) collective-permute-start(f32[1,32,128]{2,1,0:T(8,128)S(1)} %get-tuple-element.39), channel_id=1, source_target_pairs={{0,8},{8,16},{16,24},{24,32},{32,40},{40,48},{48,56},{56,64},{64,7... | collective-permute-start | bytes 49160 | tf_op jit(solution)/shard_map/ppermute | solution.py:282
  45.7 3.9 %collective-permute-start.7 = (f32[10,1,128]{2,1,0:T(1,128)S(1)}, f32[10,1,128]{2,1,0:T(1,128)S(1)}, u32[]{:S(2)}, u32[]{:S(2)}) collective-permute-start(f32[10,1,128]{2,1,0:T(1,128)S(1)} %get-tuple-element.26), channel_id=1, source_target_pairs={{1,0},{2,1},{3,2},{4,3},{5,4},{6,5},{7,6},{9,8},{10,9},{11,10},{12... | collective-permute-start | bytes 15368 | tf_op jit(solution)/shard_map/ppermute | solution.py:285
  49.6 3.0 %collective-permute-start.6 = (f32[10,1,128]{2,1,0:T(1,128)S(1)}, f32[10,1,128]{2,1,0:T(1,128)S(1)}, u32[]{:S(2)}, u32[]{:S(2)}) collective-permute-start(f32[10,1,128]{2,1,0:T(1,128)S(1)} %get-tuple-element.25), channel_id=1, source_target_pairs={{0,1},{1,2},{2,3},{3,4},{4,5},{5,6},{6,7},{8,9},{9,10},{10,11},{11... | collective-permute-start | bytes 15368 | tf_op jit(solution)/shard_map/ppermute | solution.py:282
  56.9 7.2 %collective-permute-start.8 = (f32[1,32,128]{2,1,0:T(8,128)S(1)}, f32[1,32,128]{2,1,0:T(8,128)S(1)}, u32[]{:S(2)}, u32[]{:S(2)}) collective-permute-start(f32[1,32,128]{2,1,0:T(8,128)S(1)} %get-tuple-element.37), channel_id=1, source_target_pairs={{0,8},{8,16},{16,24},{24,32},{32,40},{40,48},{48,56},{56,64},{64,7... | collective-permute-start | bytes 49160 | tf_op jit(solution)/shard_map/ppermute | solution.py:282
  64.7 6.8 %all-to-all-start = ((s32[32,1,256]{2,1,0:T(1,128)}), s32[32,1,256]{2,1,0:T(1,128)S(1)}, u32[]{:S(2)}, u32[]{:S(2)}) async-start(s32[32,1,256]{2,1,0:T(1,128)} %all_to_all.17), calls=%async_computation | async-start | bytes 65536 | tf_op jit(solution)/shard_map/all_to_all | solution.py:328
  71.6 3.9 %collective-permute-start.11 = (f32[10,1,128]{2,1,0:T(1,128)S(1)}, f32[10,1,128]{2,1,0:T(1,128)S(1)}, u32[]{:S(2)}, u32[]{:S(2)}) collective-permute-start(f32[10,1,128]{2,1,0:T(1,128)S(1)} %get-tuple-element.22), channel_id=1, source_target_pairs={{1,0},{2,1},{3,2},{4,3},{5,4},{6,5},{7,6},{9,8},{10,9},{11,10},{12... | collective-permute-start | bytes 15368 | tf_op jit(solution)/shard_map/ppermute | solution.py:285
  75.5 3.0 %collective-permute-start.10 = (f32[10,1,128]{2,1,0:T(1,128)S(1)}, f32[10,1,128]{2,1,0:T(1,128)S(1)}, u32[]{:S(2)}, u32[]{:S(2)}) collective-permute-start(f32[10,1,128]{2,1,0:T(1,128)S(1)} %get-tuple-element.21), channel_id=1, source_target_pairs={{0,1},{1,2},{2,3},{3,4},{4,5},{5,6},{6,7},{8,9},{9,10},{10,11},{11... | collective-permute-start | bytes 15368 | tf_op jit(solution)/shard_map/ppermute | solution.py:282
  78.6 6.1 %shard_map.73.unknown_ref = s32[256,128]{1,0:T(8,128)S(1)} custom-call(s32[256,128]{1,0:T(8,128)S(1)} %bitcast.240, s32[64,128]{1,0:T(8,128)S(1)} %bitcast.245), custom_call_target="tpu_custom_call" | custom-call | tf_op jit(solution)/shard_map/pallas_call | solution.py:55
  85.0 2.7 %fusion.98 = f32[8,32,128]{2,1,0:T(8,128)S(1)} fusion(f32[8,32,128]{2,1,0:T(8,128)S(1)} %copy-done.5, f32[10,34,130]{2,1,0:T(8,128)S(1)} %select_maximum_fusion.12, f32[10,33,128]{2,1,0:T(8,128)S(1)} %get-tuple-element.20, f32[1,32,128]{2,1,0:T(8,128)S(1)} %collective-permute-done.9, f32[8,32,128]{2,1,0:T(8,128)S(1)} %fusion.130, ...), kind=kLoop, calls=%fused_computation.215 | loop fusion | flops 1835008 | bytes 7110656 | tf_op jit(solution)/shard_map/sub | solution.py:334
  87.7 8.1 %shard_map.76 = f32[32,128]{1,0:T(8,128)S(1)} custom-call(s32[256,128]{1,0:T(8,128)S(1)} %bitcast.241, s32[256,128]{1,0:T(8,128)S(1)} %shard_map.73.unknown_ref, f32[256,128]{1,0:T(8,128)S(1)} %bitcast.243), custom_call_target="tpu_custom_call" | custom-call | tf_op jit(solution)/shard_map/pallas_call | solution.py:78
  95.8 13.5 %all_to_all.26 = f32[32,1,128]{2,1,0:T(1,128)S(1)} all-to-all(f32[32,1,128]{2,1,0:T(1,128)S(1)} %bitcast.247), channel_id=1, replica_groups=mesh['slab'=32,'col'=8] {'slab'}, dimensions={0} | all-to-all | bytes 32768 | tf_op jit(solution)/shard_map/all_to_all | solution.py:336
  109.9 7.8 %all-to-all-start.2 = ((f32[32,1,128]{2,1,0:T(1,128)}), f32[32,1,128]{2,1,0:T(1,128)S(1)}, u32[]{:S(2)}, u32[]{:S(2)}) async-start(f32[32,1,128]{2,1,0:T(1,128)} %broadcast_in_dim.10), calls=%async_computation.2 | async-start | bytes 32768 | tf_op jit(solution)/shard_map/all_to_all | solution.py:338
  117.8 2.7 %fusion.190 = (f32[32,128,128]{2,1,0:T(8,128)S(1)}, f32[32,128,128]{2,1,0:T(8,128)S(1)}) fusion(f32[32,256,128]{2,1,0:T(8,128)} %bitcast.248), kind=kLoop, calls=%fused_computation.413 | loop fusion | bytes 8388608 | tf_op jit(solution)/shard_map/slice | solution.py:342
  120.5 25.2 %shard_map.75.factor_ref = f32[32,384,128]{2,1,0:T(8,128)} custom-call(f32[32,128,128]{2,1,0:T(8,128)S(1)} %get-tuple-element.6.diag_ref, f32[32,128,128]{2,1,0:T(8,128)S(1)} %get-tuple-element.5.lower_ref), custom_call_target="tpu_custom_call" | custom-call | tf_op jit(solution)/shard_map/pallas_call | solution.py:228
  145.7 2.8 %copy-done = f32[32,384,128]{2,1,0:T(8,128)S(1)} copy-done((f32[32,384,128]{2,1,0:T(8,128)S(1)}, f32[32,384,128]{2,1,0:T(8,128)}, u32[]{:S(2)}) %copy-start) | copy-done | bytes 6291480
  148.5 4.6 %shard_map.77.table_ref = f32[32,128]{1,0:T(8,128)S(1)} custom-call(f32[32,384,128]{2,1,0:T(8,128)S(1)} %copy-done, f32[32,128]{1,0:T(8,128)S(1)} %bitcast.246), custom_call_target="tpu_custom_call" | custom-call | tf_op jit(solution)/shard_map/pallas_call | solution.py:266
  153.1 6.2 %shard_map.78 = f32[256,128]{1,0:T(8,128)S(1)} custom-call(s32[256,128]{1,0:T(8,128)S(1)} %bitcast.242, s32[256,128]{1,0:T(8,128)S(1)} %shard_map.73.unknown_ref, f32[32,128]{1,0:T(8,128)S(1)} %shard_map.77.table_ref, f32[256,128]{1,0:T(8,128)S(1)} %bitcast.235), custom_call_target="tpu_custom_call" | custom-call | tf_op jit(solution)/shard_map/pallas_call | solution.py:94
  159.3 2.5 %collective-permute-start.13 = (f32[1,32,128]{2,1,0:T(8,128)S(1)}, f32[1,32,128]{2,1,0:T(8,128)S(1)}, u32[]{:S(2)}, u32[]{:S(2)}) collective-permute-start(f32[1,32,128]{2,1,0:T(8,128)S(1)} %get-tuple-element.36), channel_id=1, source_target_pairs={{8,0},{16,8},{24,16},{32,24},{40,32},{48,40},{56,48},{64,56},{72,6... | collective-permute-start | bytes 49160 | tf_op jit(solution)/shard_map/ppermute | solution.py:285
  161.7 6.1 %collective-permute-start.12 = (f32[1,32,128]{2,1,0:T(8,128)S(1)}, f32[1,32,128]{2,1,0:T(8,128)S(1)}, u32[]{:S(2)}, u32[]{:S(2)}) collective-permute-start(f32[1,32,128]{2,1,0:T(8,128)S(1)} %get-tuple-element.35), channel_id=1, source_target_pairs={{0,8},{8,16},{16,24},{24,32},{32,40},{40,48},{48,56},{56,64},{64,7... | collective-permute-start | bytes 49160 | tf_op jit(solution)/shard_map/ppermute | solution.py:282
  168.7 4.9 %collective-permute-start.15 = (f32[10,1,128]{2,1,0:T(1,128)S(1)}, f32[10,1,128]{2,1,0:T(1,128)S(1)}, u32[]{:S(2)}, u32[]{:S(2)}) collective-permute-start(f32[10,1,128]{2,1,0:T(1,128)S(1)} %get-tuple-element.18), channel_id=1, source_target_pairs={{1,0},{2,1},{3,2},{4,3},{5,4},{6,5},{7,6},{9,8},{10,9},{11,10},{12... | collective-permute-start | bytes 15368 | tf_op jit(solution)/shard_map/ppermute | solution.py:285
  173.6 2.9 %collective-permute-start.14 = (f32[10,1,128]{2,1,0:T(1,128)S(1)}, f32[10,1,128]{2,1,0:T(1,128)S(1)}, u32[]{:S(2)}, u32[]{:S(2)}) collective-permute-start(f32[10,1,128]{2,1,0:T(1,128)S(1)} %get-tuple-element.17), channel_id=1, source_target_pairs={{0,1},{1,2},{2,3},{3,4},{4,5},{5,6},{6,7},{8,9},{9,10},{10,11},{11... | collective-permute-start | bytes 15368 | tf_op jit(solution)/shard_map/ppermute | solution.py:282
  180.7 7.2 %collective-permute-start.16 = (f32[1,32,128]{2,1,0:T(8,128)S(1)}, f32[1,32,128]{2,1,0:T(8,128)S(1)}, u32[]{:S(2)}, u32[]{:S(2)}) collective-permute-start(f32[1,32,128]{2,1,0:T(8,128)S(1)} %get-tuple-element.33), channel_id=1, source_target_pairs={{0,8},{8,16},{16,24},{24,32},{32,40},{40,48},{48,56},{56,64},{64,7... | collective-permute-start | bytes 49160 | tf_op jit(solution)/shard_map/ppermute | solution.py:282
  188.8 4.0 %collective-permute-start.19 = (f32[10,1,128]{2,1,0:T(1,128)S(1)}, f32[10,1,128]{2,1,0:T(1,128)S(1)}, u32[]{:S(2)}, u32[]{:S(2)}) collective-permute-start(f32[10,1,128]{2,1,0:T(1,128)S(1)} %get-tuple-element.14), channel_id=1, source_target_pairs={{1,0},{2,1},{3,2},{4,3},{5,4},{6,5},{7,6},{9,8},{10,9},{11,10},{12... | collective-permute-start | bytes 15368 | tf_op jit(solution)/shard_map/ppermute | solution.py:285
  192.9 2.9 %collective-permute-start.18 = (f32[10,1,128]{2,1,0:T(1,128)S(1)}, f32[10,1,128]{2,1,0:T(1,128)S(1)}, u32[]{:S(2)}, u32[]{:S(2)}) collective-permute-start(f32[10,1,128]{2,1,0:T(1,128)S(1)} %get-tuple-element.13), channel_id=1, source_target_pairs={{0,1},{1,2},{2,3},{3,4},{4,5},{5,6},{6,7},{8,9},{9,10},{10,11},{11... | collective-permute-start | bytes 15368 | tf_op jit(solution)/shard_map/ppermute | solution.py:282
  200.0 7.2 %collective-permute-start.20 = (f32[1,32,128]{2,1,0:T(8,128)S(1)}, f32[1,32,128]{2,1,0:T(8,128)S(1)}, u32[]{:S(2)}, u32[]{:S(2)}) collective-permute-start(f32[1,32,128]{2,1,0:T(8,128)S(1)} %get-tuple-element.31), channel_id=1, source_target_pairs={{0,8},{8,16},{16,24},{24,32},{32,40},{40,48},{48,56},{56,64},{64,7... | collective-permute-start | bytes 49160 | tf_op jit(solution)/shard_map/ppermute | solution.py:282
  208.1 4.0 %collective-permute-start.23 = (f32[10,1,128]{2,1,0:T(1,128)S(1)}, f32[10,1,128]{2,1,0:T(1,128)S(1)}, u32[]{:S(2)}, u32[]{:S(2)}) collective-permute-start(f32[10,1,128]{2,1,0:T(1,128)S(1)} %get-tuple-element.10), channel_id=1, source_target_pairs={{1,0},{2,1},{3,2},{4,3},{5,4},{6,5},{7,6},{9,8},{10,9},{11,10},{12... | collective-permute-start | bytes 15368 | tf_op jit(solution)/shard_map/ppermute | solution.py:285
  212.1 2.9 %collective-permute-start.22 = (f32[10,1,128]{2,1,0:T(1,128)S(1)}, f32[10,1,128]{2,1,0:T(1,128)S(1)}, u32[]{:S(2)}, u32[]{:S(2)}) collective-permute-start(f32[10,1,128]{2,1,0:T(1,128)S(1)} %get-tuple-element.9), channel_id=1, source_target_pairs={{0,1},{1,2},{2,3},{3,4},{4,5},{5,6},{6,7},{8,9},{9,10},{10,11},{11... | collective-permute-start | bytes 15368 | tf_op jit(solution)/shard_map/ppermute | solution.py:282
  (82 shorter events, 31.8 us)
Async XLA Ops:
  6.5 111.3 %all-gather.3.cloned.1.call-start = ((), (), s32[]{:S(2)}) async-start(), calls=%async_computation.3 | async-start | bytes 4325376 | tf_op jit(solution)/shard_map/all_gather | solution.py:326
  14.3 8.6 %collective-permute-start.1 = (f32[1,32,128]{2,1,0:T(8,128)S(1)}, f32[1,32,128]{2,1,0:T(8,128)S(1)}, u32[]{:S(2)}, u32[]{:S(2)}) collective-permute-start(f32[1,32,128]{2,1,0:T(8,128)S(1)} %get-tuple-element.42), channel_id=1, source_target_pairs={{8,0},{16,8},{24,16},{32,24},{40,32},{48,40},{56,48},{64,56},{72,6... | collective-permute-start | bytes 49160 | tf_op jit(solution)/shard_map/ppermute | solution.py:285
  17.0 6.8 %collective-permute-start = (f32[1,32,128]{2,1,0:T(8,128)S(1)}, f32[1,32,128]{2,1,0:T(8,128)S(1)}, u32[]{:S(2)}, u32[]{:S(2)}) collective-permute-start(f32[1,32,128]{2,1,0:T(8,128)S(1)} %get-tuple-element.41), channel_id=1, source_target_pairs={{0,8},{8,16},{16,24},{24,32},{32,40},{40,48},{48,56},{56,64},{64,7... | collective-permute-start | bytes 49160 | tf_op jit(solution)/shard_map/ppermute | solution.py:282
  23.8 7.0 %collective-permute-start.3 = (f32[10,1,128]{2,1,0:T(1,128)S(1)}, f32[10,1,128]{2,1,0:T(1,128)S(1)}, u32[]{:S(2)}, u32[]{:S(2)}) collective-permute-start(f32[10,1,128]{2,1,0:T(1,128)S(1)} %get-tuple-element.30), channel_id=1, source_target_pairs={{1,0},{2,1},{3,2},{4,3},{5,4},{6,5},{7,6},{9,8},{10,9},{11,10},{12... | collective-permute-start | bytes 15368 | tf_op jit(solution)/shard_map/ppermute | solution.py:285
  27.8 3.8 %collective-permute-start.2 = (f32[10,1,128]{2,1,0:T(1,128)S(1)}, f32[10,1,128]{2,1,0:T(1,128)S(1)}, u32[]{:S(2)}, u32[]{:S(2)}) collective-permute-start(f32[10,1,128]{2,1,0:T(1,128)S(1)} %get-tuple-element.29), channel_id=1, source_target_pairs={{0,1},{1,2},{2,3},{3,4},{4,5},{5,6},{6,7},{8,9},{9,10},{10,11},{11... | collective-permute-start | bytes 15368 | tf_op jit(solution)/shard_map/ppermute | solution.py:282
  31.8 21.8 %copy-start.3 = (f32[27,8,32,128]{3,2,1,0:T(8,128)S(1)}, f32[27,8,32,128]{3,2,1,0:T(8,128)}, u32[]{:S(2)}) copy-start(f32[27,8,32,128]{3,2,1,0:T(8,128)} %param.8) | copy-start | bytes 10616836
  31.8 21.8 %copy-start.5 = (f32[8,32,128]{2,1,0:T(8,128)S(1)}, f32[8,32,128]{2,1,0:T(8,128)}, u32[]{:S(2)}) copy-start(f32[8,32,128]{2,1,0:T(8,128)} %param.7) | copy-start | bytes 393220
  35.6 9.2 %collective-permute-start.5 = (f32[1,32,128]{2,1,0:T(8,128)S(1)}, f32[1,32,128]{2,1,0:T(8,128)S(1)}, u32[]{:S(2)}, u32[]{:S(2)}) collective-permute-start(f32[1,32,128]{2,1,0:T(8,128)S(1)} %get-tuple-element.40), channel_id=1, source_target_pairs={{8,0},{16,8},{24,16},{32,24},{40,32},{48,40},{56,48},{64,56},{72,6... | collective-permute-start | bytes 49160 | tf_op jit(solution)/shard_map/ppermute | solution.py:285
  37.6 8.1 %collective-permute-start.4 = (f32[1,32,128]{2,1,0:T(8,128)S(1)}, f32[1,32,128]{2,1,0:T(8,128)S(1)}, u32[]{:S(2)}, u32[]{:S(2)}) collective-permute-start(f32[1,32,128]{2,1,0:T(8,128)S(1)} %get-tuple-element.39), channel_id=1, source_target_pairs={{0,8},{8,16},{16,24},{24,32},{32,40},{40,48},{48,56},{56,64},{64,7... | collective-permute-start | bytes 49160 | tf_op jit(solution)/shard_map/ppermute | solution.py:282
  45.7 7.0 %collective-permute-start.7 = (f32[10,1,128]{2,1,0:T(1,128)S(1)}, f32[10,1,128]{2,1,0:T(1,128)S(1)}, u32[]{:S(2)}, u32[]{:S(2)}) collective-permute-start(f32[10,1,128]{2,1,0:T(1,128)S(1)} %get-tuple-element.26), channel_id=1, source_target_pairs={{1,0},{2,1},{3,2},{4,3},{5,4},{6,5},{7,6},{9,8},{10,9},{11,10},{12... | collective-permute-start | bytes 15368 | tf_op jit(solution)/shard_map/ppermute | solution.py:285
  49.6 3.8 %collective-permute-start.6 = (f32[10,1,128]{2,1,0:T(1,128)S(1)}, f32[10,1,128]{2,1,0:T(1,128)S(1)}, u32[]{:S(2)}, u32[]{:S(2)}) collective-permute-start(f32[10,1,128]{2,1,0:T(1,128)S(1)} %get-tuple-element.25), channel_id=1, source_target_pairs={{0,1},{1,2},{2,3},{3,4},{4,5},{5,6},{6,7},{8,9},{9,10},{10,11},{11... | collective-permute-start | bytes 15368 | tf_op jit(solution)/shard_map/ppermute | solution.py:282
  53.6 10.5 %copy-start.6 = (s32[1,1,32,256]{3,2,1,0:T(8,128)S(1)}, s32[1,1,32,256]{3,2,1,0:T(8,128)}, u32[]{:S(2)}) copy-start(s32[1,1,32,256]{3,2,1,0:T(8,128)} %param.11) | copy-start | bytes 98308
  53.7 24.9 %copy-start.1 = (s32[8,32,128]{2,1,0:T(8,128)S(1)}, s32[8,32,128]{2,1,0:T(8,128)}, u32[]{:S(2)}) copy-start(s32[8,32,128]{2,1,0:T(8,128)} %param.10) | copy-start | bytes 393220
  54.9 16.6 %collective-permute-start.9 = (f32[1,32,128]{2,1,0:T(8,128)S(1)}, f32[1,32,128]{2,1,0:T(8,128)S(1)}, u32[]{:S(2)}, u32[]{:S(2)}) collective-permute-start(f32[1,32,128]{2,1,0:T(8,128)S(1)} %get-tuple-element.38), channel_id=1, source_target_pairs={{8,0},{16,8},{24,16},{32,24},{40,32},{48,40},{56,48},{64,56},{72,6... | collective-permute-start | bytes 49160 | tf_op jit(solution)/shard_map/ppermute | solution.py:285
  56.9 14.7 %collective-permute-start.8 = (f32[1,32,128]{2,1,0:T(8,128)S(1)}, f32[1,32,128]{2,1,0:T(8,128)S(1)}, u32[]{:S(2)}, u32[]{:S(2)}) collective-permute-start(f32[1,32,128]{2,1,0:T(8,128)S(1)} %get-tuple-element.37), channel_id=1, source_target_pairs={{0,8},{8,16},{16,24},{24,32},{32,40},{40,48},{48,56},{56,64},{64,7... | collective-permute-start | bytes 49160 | tf_op jit(solution)/shard_map/ppermute | solution.py:282
  64.7 13.8 %all-to-all-start = ((s32[32,1,256]{2,1,0:T(1,128)}), s32[32,1,256]{2,1,0:T(1,128)S(1)}, u32[]{:S(2)}, u32[]{:S(2)}) async-start(s32[32,1,256]{2,1,0:T(1,128)} %all_to_all.17), calls=%async_computation | async-start | bytes 65536 | tf_op jit(solution)/shard_map/all_to_all | solution.py:328
  71.6 13.1 %collective-permute-start.11 = (f32[10,1,128]{2,1,0:T(1,128)S(1)}, f32[10,1,128]{2,1,0:T(1,128)S(1)}, u32[]{:S(2)}, u32[]{:S(2)}) collective-permute-start(f32[10,1,128]{2,1,0:T(1,128)S(1)} %get-tuple-element.22), channel_id=1, source_target_pairs={{1,0},{2,1},{3,2},{4,3},{5,4},{6,5},{7,6},{9,8},{10,9},{11,10},{12... | collective-permute-start | bytes 15368 | tf_op jit(solution)/shard_map/ppermute | solution.py:285
  75.5 9.2 %collective-permute-start.10 = (f32[10,1,128]{2,1,0:T(1,128)S(1)}, f32[10,1,128]{2,1,0:T(1,128)S(1)}, u32[]{:S(2)}, u32[]{:S(2)}) collective-permute-start(f32[10,1,128]{2,1,0:T(1,128)S(1)} %get-tuple-element.21), channel_id=1, source_target_pairs={{0,1},{1,2},{2,3},{3,4},{4,5},{5,6},{6,7},{8,9},{9,10},{10,11},{11... | collective-permute-start | bytes 15368 | tf_op jit(solution)/shard_map/ppermute | solution.py:282
  109.9 35.8 %all-to-all-start.2 = ((f32[32,1,128]{2,1,0:T(1,128)}), f32[32,1,128]{2,1,0:T(1,128)S(1)}, u32[]{:S(2)}, u32[]{:S(2)}) async-start(f32[32,1,128]{2,1,0:T(1,128)} %broadcast_in_dim.10), calls=%async_computation.2 | async-start | bytes 32768 | tf_op jit(solution)/shard_map/all_to_all | solution.py:338
  148.5 29.1 %copy-start.4 = (f32[27,8,32,128]{3,2,1,0:T(8,128)S(1)}, f32[27,8,32,128]{3,2,1,0:T(8,128)}, u32[]{:S(2)}) copy-start(f32[27,8,32,128]{3,2,1,0:T(8,128)} %param.8) | copy-start | bytes 10616836
  159.3 8.6 %collective-permute-start.13 = (f32[1,32,128]{2,1,0:T(8,128)S(1)}, f32[1,32,128]{2,1,0:T(8,128)S(1)}, u32[]{:S(2)}, u32[]{:S(2)}) collective-permute-start(f32[1,32,128]{2,1,0:T(8,128)S(1)} %get-tuple-element.36), channel_id=1, source_target_pairs={{8,0},{16,8},{24,16},{32,24},{40,32},{48,40},{56,48},{64,56},{72,6... | collective-permute-start | bytes 49160 | tf_op jit(solution)/shard_map/ppermute | solution.py:285
  161.7 7.0 %collective-permute-start.12 = (f32[1,32,128]{2,1,0:T(8,128)S(1)}, f32[1,32,128]{2,1,0:T(8,128)S(1)}, u32[]{:S(2)}, u32[]{:S(2)}) collective-permute-start(f32[1,32,128]{2,1,0:T(8,128)S(1)} %get-tuple-element.35), channel_id=1, source_target_pairs={{0,8},{8,16},{16,24},{24,32},{32,40},{40,48},{48,56},{56,64},{64,7... | collective-permute-start | bytes 49160 | tf_op jit(solution)/shard_map/ppermute | solution.py:282
  168.7 7.8 %collective-permute-start.15 = (f32[10,1,128]{2,1,0:T(1,128)S(1)}, f32[10,1,128]{2,1,0:T(1,128)S(1)}, u32[]{:S(2)}, u32[]{:S(2)}) collective-permute-start(f32[10,1,128]{2,1,0:T(1,128)S(1)} %get-tuple-element.18), channel_id=1, source_target_pairs={{1,0},{2,1},{3,2},{4,3},{5,4},{6,5},{7,6},{9,8},{10,9},{11,10},{12... | collective-permute-start | bytes 15368 | tf_op jit(solution)/shard_map/ppermute | solution.py:285
  173.6 3.7 %collective-permute-start.14 = (f32[10,1,128]{2,1,0:T(1,128)S(1)}, f32[10,1,128]{2,1,0:T(1,128)S(1)}, u32[]{:S(2)}, u32[]{:S(2)}) collective-permute-start(f32[10,1,128]{2,1,0:T(1,128)S(1)} %get-tuple-element.17), channel_id=1, source_target_pairs={{0,1},{1,2},{2,3},{3,4},{4,5},{5,6},{6,7},{8,9},{9,10},{10,11},{11... | collective-permute-start | bytes 15368 | tf_op jit(solution)/shard_map/ppermute | solution.py:282
  178.8 9.2 %collective-permute-start.17 = (f32[1,32,128]{2,1,0:T(8,128)S(1)}, f32[1,32,128]{2,1,0:T(8,128)S(1)}, u32[]{:S(2)}, u32[]{:S(2)}) collective-permute-start(f32[1,32,128]{2,1,0:T(8,128)S(1)} %get-tuple-element.34), channel_id=1, source_target_pairs={{8,0},{16,8},{24,16},{32,24},{40,32},{48,40},{56,48},{64,56},{72,6... | collective-permute-start | bytes 49160 | tf_op jit(solution)/shard_map/ppermute | solution.py:285
  180.7 8.1 %collective-permute-start.16 = (f32[1,32,128]{2,1,0:T(8,128)S(1)}, f32[1,32,128]{2,1,0:T(8,128)S(1)}, u32[]{:S(2)}, u32[]{:S(2)}) collective-permute-start(f32[1,32,128]{2,1,0:T(8,128)S(1)} %get-tuple-element.33), channel_id=1, source_target_pairs={{0,8},{8,16},{16,24},{24,32},{32,40},{40,48},{48,56},{56,64},{64,7... | collective-permute-start | bytes 49160 | tf_op jit(solution)/shard_map/ppermute | solution.py:282
  188.8 7.0 %collective-permute-start.19 = (f32[10,1,128]{2,1,0:T(1,128)S(1)}, f32[10,1,128]{2,1,0:T(1,128)S(1)}, u32[]{:S(2)}, u32[]{:S(2)}) collective-permute-start(f32[10,1,128]{2,1,0:T(1,128)S(1)} %get-tuple-element.14), channel_id=1, source_target_pairs={{1,0},{2,1},{3,2},{4,3},{5,4},{6,5},{7,6},{9,8},{10,9},{11,10},{12... | collective-permute-start | bytes 15368 | tf_op jit(solution)/shard_map/ppermute | solution.py:285
  192.9 3.7 %collective-permute-start.18 = (f32[10,1,128]{2,1,0:T(1,128)S(1)}, f32[10,1,128]{2,1,0:T(1,128)S(1)}, u32[]{:S(2)}, u32[]{:S(2)}) collective-permute-start(f32[10,1,128]{2,1,0:T(1,128)S(1)} %get-tuple-element.13), channel_id=1, source_target_pairs={{0,1},{1,2},{2,3},{3,4},{4,5},{5,6},{6,7},{8,9},{9,10},{10,11},{11... | collective-permute-start | bytes 15368 | tf_op jit(solution)/shard_map/ppermute | solution.py:282
  198.0 9.2 %collective-permute-start.21 = (f32[1,32,128]{2,1,0:T(8,128)S(1)}, f32[1,32,128]{2,1,0:T(8,128)S(1)}, u32[]{:S(2)}, u32[]{:S(2)}) collective-permute-start(f32[1,32,128]{2,1,0:T(8,128)S(1)} %get-tuple-element.32), channel_id=1, source_target_pairs={{8,0},{16,8},{24,16},{32,24},{40,32},{48,40},{56,48},{64,56},{72,6... | collective-permute-start | bytes 49160 | tf_op jit(solution)/shard_map/ppermute | solution.py:285
  200.0 8.1 %collective-permute-start.20 = (f32[1,32,128]{2,1,0:T(8,128)S(1)}, f32[1,32,128]{2,1,0:T(8,128)S(1)}, u32[]{:S(2)}, u32[]{:S(2)}) collective-permute-start(f32[1,32,128]{2,1,0:T(8,128)S(1)} %get-tuple-element.31), channel_id=1, source_target_pairs={{0,8},{8,16},{16,24},{24,32},{32,40},{40,48},{48,56},{56,64},{64,7... | collective-permute-start | bytes 49160 | tf_op jit(solution)/shard_map/ppermute | solution.py:282
  208.1 7.0 %collective-permute-start.23 = (f32[10,1,128]{2,1,0:T(1,128)S(1)}, f32[10,1,128]{2,1,0:T(1,128)S(1)}, u32[]{:S(2)}, u32[]{:S(2)}) collective-permute-start(f32[10,1,128]{2,1,0:T(1,128)S(1)} %get-tuple-element.10), channel_id=1, source_target_pairs={{1,0},{2,1},{3,2},{4,3},{5,4},{6,5},{7,6},{9,8},{10,9},{11,10},{12... | collective-permute-start | bytes 15368 | tf_op jit(solution)/shard_map/ppermute | solution.py:285
  212.1 3.7 %collective-permute-start.22 = (f32[10,1,128]{2,1,0:T(1,128)S(1)}, f32[10,1,128]{2,1,0:T(1,128)S(1)}, u32[]{:S(2)}, u32[]{:S(2)}) collective-permute-start(f32[10,1,128]{2,1,0:T(1,128)S(1)} %get-tuple-element.9), channel_id=1, source_target_pairs={{0,1},{1,2},{2,3},{3,4},{4,5},{5,6},{6,7},{8,9},{9,10},{10,11},{11... | collective-permute-start | bytes 15368 | tf_op jit(solution)/shard_map/ppermute | solution.py:282
  (2 other events, 3.6 us)
Sparse Core Ops, SparseCore 0:
  11.2 78.0 all-gather.2

commit v2 on v1

--- a/solution.py
+++ b/solution.py
@@ -9,6 +9,7 @@
 
 F32 = jnp.float32
 BF16 = jnp.bfloat16
+ROWS = 40
 
 
 def nn(a, b):
@@ -29,7 +30,6 @@
     return jnp.concatenate([block[first : first + 1], block[first + 1 : first + 2]], axis=1)
 
 def gather_rows(table, height, parts, high, low):
-
     rows = []
     for first in range(0, 8, 2):
         picked = nn(table, one_hot(pair(low, first), 128))
@@ -42,7 +42,7 @@
     return jnp.concatenate(rows, axis=0)
 
 def lookup_kernel(slot_ref, table_ref, out_ref):
-    table = table_ref[...].astype(F32).astype(BF16)
+    table = table_ref[...].astype(BF16)
 
     @pl.loop(0, slot_ref.shape[0] // 8)
     def _(block):
@@ -58,28 +58,49 @@
         compiler_params=pltpu.CompilerParams(vmem_limit_bytes=16 * 2**20),
     )(slot, table)
 
-def scatter_kernel(slot_ref, unknown_ref, value_ref, out_ref):
+def scatter_kernel(slot_ref, value_ref, out_ref):
     def step(block, total):
         where = pl.ds(pl.multiple_of(block * 8, 8), 8)
-        owner = slot_ref[where] >> 8
-        unknown = unknown_ref[where]
+        slot = slot_ref[where]
+        high_slot, low_slot = slot >> 7, slot & 127
         value = value_ref[where]
         for first in range(0, 8, 2):
-            mask = lax.broadcasted_iota(jnp.int32, (32, 256), 0) == pair(owner, first)
+            mask = lax.broadcasted_iota(jnp.int32, (64, 256), 0) == pair(high_slot, first)
             spread = jnp.where(mask, pair(value, first), 0.0)
             high, low = split(spread)
-            total = total + nt(jnp.concatenate([high, low], axis=0), one_hot(pair(unknown, first), 128))
+            total = total + nt(jnp.concatenate([high, low], axis=0), one_hot(pair(low_slot, first), 128))
         return total
 
-    total = lax.fori_loop(0, slot_ref.shape[0] // 8, step, jnp.zeros((64, 128), F32))
-    out_ref[...] = total[:32] + total[32:]
-
-def scatter(slot, unknown, value):
+    total = lax.fori_loop(0, slot_ref.shape[0] // 8, step, jnp.zeros((128, 128), F32))
+    out_ref[...] = total[:64] + total[64:]
+
+
+def scatter(slot, value):
     return pl.pallas_call(
         scatter_kernel,
+        out_shape=jax.ShapeDtypeStruct((64, 128), F32),
+        compiler_params=pltpu.CompilerParams(vmem_limit_bytes=16 * 2**20),
+    )(slot, value)
+
+
+def collect_kernel(index_ref, value_ref, out_ref):
+    total = jnp.zeros((16, 128), F32)
+    for first in range(0, 64, 2):
+        row = pair(value_ref[...], first)
+        high, low = split(jnp.concatenate([row] * 8, axis=0))
+        spread = jnp.concatenate([high, low], axis=0)
+        total = total + nt(spread, one_hot(pair(index_ref[...], first), 128))
+    row = total[0:1] + total[8:9]
+    out_ref[...] = jnp.concatenate([row] * 32, axis=0)
+
+
+def collect(index, value):
+    return pl.pallas_call(
+        collect_kernel,
         out_shape=jax.ShapeDtypeStruct((32, 128), F32),
         compiler_params=pltpu.CompilerParams(vmem_limit_bytes=16 * 2**20),
-    )(slot, unknown, value)
+    )(index, value)
+
 
 def gather_kernel(slot_ref, unknown_ref, table_ref, base_ref, out_ref):
     high, low = split(table_ref[...])
@@ -110,7 +131,6 @@
     return jnp.max(jnp.sum(jnp.abs(e), axis=0, keepdims=True))
 
 def invert(count, get_a, x_ref, r_ref):
-
     n = 128
     rows = lax.broadcasted_iota(jnp.int32, (n, n), 0)
     cols = lax.broadcasted_iota(jnp.int32, (n, n), 1)
@@ -192,7 +212,9 @@
         compiler_params=pltpu.CompilerParams(vmem_limit_bytes=16 * 2**20),
     )(a)
 
-def factor_kernel(count, diag_ref, lower_ref, out_ref, d_ref, l_ref, x_ref, r_ref):
+def factor_kernel(count, every_ref, out_ref, d_ref, l_ref, x_ref, r_ref):
+    diag_ref = every_ref.at[:, 0:128]
+    lower_ref = every_ref.at[:, 128:256]
     stride = 1
     while stride < count:
         gone = list(range(stride, count, 2 * stride))
@@ -222,9 +244,8 @@
     out_ref[0, 0:128] = x_ref[0]
     out_ref[0, 128:384] = jnp.zeros((256, 128), F32)
 
-def factor(diag, lower):
-
-    count = diag.shape[0]
+def factor(every):
+    count = every.shape[0]
     return pl.pallas_call(
         functools.partial(factor_kernel, count),
         out_shape=jax.ShapeDtypeStruct((count, 384, 128), F32),
@@ -235,7 +256,7 @@
             pltpu.VMEM((count // 4, 128, 128), F32),
         ],
         compiler_params=pltpu.CompilerParams(vmem_limit_bytes=48 * 2**20),
-    )(diag, lower)
+    )(every)
 
 def solve_kernel(count, factor_ref, rhs_ref, out_ref, r_ref):
     def row3(form, row, mat):
@@ -271,78 +292,262 @@
     )(factors, rhs)
 
 
+def cut_kernel(weights_ref, side_ref, next_ref, previous_ref, start_ref):
+    for offset in range(27):
+        for x in range(8):
+            next_ref[8 * offset + x] = weights_ref[offset, x, 30:32]
+            previous_ref[8 * offset + x] = weights_ref[offset, x, 0:2]
+    for x in range(8):
+        start_ref[x] = side_ref[x] / weights_ref[13, x]
+        next_ref[216 + x] = side_ref[x, 30:32]
+        previous_ref[216 + x] = side_ref[x, 0:2]
+        next_ref[224 + x] = start_ref[x, 29:31]
+        next_ref[232 + x] = start_ref[x, 30:32]
+        previous_ref[224 + x] = start_ref[x, 0:2]
+        previous_ref[232 + x] = start_ref[x, 1:3]
+
+
+def cut(weights, side):
+    rows = jax.ShapeDtypeStruct((240, 2, 128), F32)
+    return pl.pallas_call(
+        cut_kernel,
+        out_shape=(rows, rows, jax.ShapeDtypeStruct((8, 32, 128), F32)),
+        compiler_params=pltpu.CompilerParams(vmem_limit_bytes=32 * 2**20),
+    )(weights, side)
+
+
+def pack_kernel(
+    weights_ref, side_ref, start_ref, left_ref, right_ref,
+    next_ref, previous_ref, edge_ref, edge_start_ref,
+):
+    edge_ref[...] = jnp.zeros((224, 8, 128), F32)
+    edge_start_ref[...] = jnp.zeros((8, 8, 128), F32)
+
+    @pl.loop(0, 224)
+    def _(k):
+        edge_ref[k, 0:2] = right_ref[k]
+        edge_ref[k, 6:8] = left_ref[k]
+
+    for x in range(8):
+        edge_start_ref[x, 0:2] = right_ref[224 + x]
+        edge_start_ref[x, 1:3] = right_ref[232 + x]
+        edge_start_ref[x, 5:7] = left_ref[224 + x]
+        edge_start_ref[x, 6:8] = left_ref[232 + x]
+
+    @pl.loop(0, 27)
+    def _(offset):
+        for x in range(2):
+            next_ref[2 * offset + x, :32] = weights_ref[offset, 6 + x]
+            next_ref[2 * offset + x, 32:] = edge_ref[8 * offset + 6 + x]
+            previous_ref[2 * offset + x, :32] = weights_ref[offset, x]
+            previous_ref[2 * offset + x, 32:] = edge_ref[8 * offset + x]
+
+    for x in range(2):
+        next_ref[54 + x, :32] = side_ref[6 + x]
+        next_ref[54 + x, 32:] = edge_ref[222 + x]
+        previous_ref[54 + x, :32] = side_ref[x]
+        previous_ref[54 + x, 32:] = edge_ref[216 + x]
+    for x in range(3):
+        next_ref[56 + x, :32] = start_ref[5 + x]
+        next_ref[56 + x, 32:] = edge_start_ref[5 + x]
+        previous_ref[56 + x, :32] = start_ref[x]
+        previous_ref[56 + x, 32:] = edge_start_ref[x]
+
+
+def pack(weights, side, start, left, right):
+    planes = jax.ShapeDtypeStruct((59, ROWS, 128), F32)
+    return pl.pallas_call(
+        pack_kernel,
+        out_shape=(
+            planes, planes,
+            jax.ShapeDtypeStruct((224, 8, 128), F32), jax.ShapeDtypeStruct((8, 8, 128), F32),
+        ),
+        compiler_params=pltpu.CompilerParams(vmem_limit_bytes=40 * 2**20),
+    )(weights, side, start, left, right)
+
+
+def shifted_planes(values_ref, shifted_ref, first, count):
+    lane = lax.broadcasted_iota(jnp.int32, (ROWS, 128), 1)
+
+    @pl.loop(first, first + count)
+    def _(x):
+        plane = values_ref[x]
+        below = jnp.where(lane == 0, 0.0, pltpu.roll(plane, 1, 1))
+        above = jnp.where(lane == 127, 0.0, pltpu.roll(plane, 127, 1))
+        for c, along_z in enumerate((below, plane, above)):
+            shifted_ref[c, x] = pltpu.roll(along_z, 1, 0)
+            shifted_ref[3 + c, x] = along_z
+            shifted_ref[6 + c, x] = pltpu.roll(along_z, ROWS - 1, 0)
+
+
+def product(weight, shifted_ref, x, begin, end):
+    total = None
+    for a in range(3):
+        for k in range(9):
+            term = weight(9 * a + k) * shifted_ref[k, x + a, begin:end]
+            total = term if total is None else total + term
+    return total
+
+
+def sweep(halo, side_ref, inverse_ref, values_ref, shifted_ref, factor, reach):
+    main_ref, edge_ref, low_ref, high_ref = halo
+    shifted_planes(values_ref, shifted_ref, 2 - reach, 10 + 2 * reach)
+
+    def update(weight, x, begin, end):
+        rest = side_ref[x, begin:end] - product(weight, shifted_ref, x, begin, end)
+        old = values_ref[x + 1, begin:end]
+        values_ref[x + 1, begin:end] = old + factor * rest * inverse_ref[x, begin:end]
+
+    for x in range(2 - reach, 2):
+        update(lambda o: low_ref[2 * o + x], x, 0, ROWS)
+    for x in range(10, 10 + reach):
+        update(lambda o: high_ref[2 * o + x - 10], x, 0, ROWS)
+
+    @pl.loop(0, 8)
+    def _(x):
+        update(lambda o: main_ref[o, x], x + 2, 0, 32)
+        if reach:
+            update(lambda o: edge_ref[8 * o + x], x + 2, 32, ROWS)
+
+
+def pre_kernel(
+    steps_ref, main_ref, edge_ref, low_ref, high_ref, side_main_ref, start_ref, edge_start_ref,
+    smooth_ref, residue_ref, side_ref, inverse_ref, values_ref, shifted_ref,
+):
+    def inverse(center):
+        return jnp.where(center > 0, 1.0 / jnp.where(center > 0, center, 1.0), 0.0)
+
+    scale = steps_ref[0]
+    for x in range(2):
+        side_ref[x] = low_ref[54 + x]
+        side_ref[10 + x] = high_ref[54 + x]
+        inverse_ref[x] = inverse(low_ref[26 + x])
+        inverse_ref[10 + x] = inverse(high_ref[26 + x])
+    for x in range(8):
+        side_ref[2 + x, :32] = side_main_ref[x]
+        side_ref[2 + x, 32:] = edge_ref[216 + x]
+        inverse_ref[2 + x, :32] = inverse(main_ref[13, x])
+        inverse_ref[2 + x, 32:] = inverse(edge_ref[104 + x])
+        values_ref[3 + x, :32] = scale * start_ref[x]
+        values_ref[3 + x, 32:] = scale * edge_start_ref[x]
+    for x in range(3):
+        values_ref[x] = scale * low_ref[56 + x]
+        values_ref[11 + x] = scale * high_ref[56 + x]
+    halo = main_ref, edge_ref, low_ref, high_ref
+    sweep(halo, side_ref, inverse_ref, values_ref, shifted_ref, steps_ref[1], 2)
+    sweep(halo, side_ref, inverse_ref, values_ref, shifted_ref, steps_ref[2], 1)
+    shifted_planes(values_ref, shifted_ref, 2, 10)
+
+    @pl.loop(0, 8)
+    def _(x):
+        smooth_ref[x] = values_ref[x + 3, :32]
+        residue_ref[x] = side_main_ref[x] - product(lambda o: main_ref[o, x], shifted_ref, x + 2, 0, 32)
+
+
+def stencil_scratch():
+    return [pltpu.VMEM((14, ROWS, 128), F32), pltpu.VMEM((9, 14, ROWS, 128), F32)]
+
+
+def pre_smooth(steps, weights, edge, low, high, side, start, edge_start):
+    cells = jax.ShapeDtypeStruct((8, 32, 128), F32)
+    outside = jax.ShapeDtypeStruct((12, ROWS, 128), F32)
+    vmem = pl.BlockSpec(memory_space=pltpu.VMEM)
+    return pl.pallas_call(
+        pre_kernel,
+        out_shape=(cells, cells, outside, outside),
+        in_specs=[pl.BlockSpec(memory_space=pltpu.SMEM)] + [vmem] * 7,
+        scratch_shapes=stencil_scratch(),
+        compiler_params=pltpu.CompilerParams(vmem_limit_bytes=40 * 2**20),
+    )(steps, weights, edge, low, high, side, start, edge_start)
+
+
+def post_kernel(
+    steps_ref, main_ref, edge_ref, low_ref, high_ref, side_ref, inverse_ref,
+    cells_ref, below_ref, beyond_ref, left_ref, right_ref,
+    out_ref, values_ref, shifted_ref,
+):
+    values_ref[:, 32:40] = jnp.zeros((14, 8, 128), F32)
+    for x in range(3):
+        values_ref[x, :32] = below_ref[x]
+        values_ref[11 + x, :32] = beyond_ref[x]
+    for x in range(8):
+        values_ref[3 + x, :32] = cells_ref[x]
+    for x in range(14):
+        values_ref[x, 32:35] = right_ref[x]
+        values_ref[x, 37:40] = left_ref[x]
+    halo = main_ref, edge_ref, low_ref, high_ref
+    sweep(halo, side_ref, inverse_ref, values_ref, shifted_ref, steps_ref[3], 2)
+    sweep(halo, side_ref, inverse_ref, values_ref, shifted_ref, steps_ref[4], 1)
+    sweep(halo, side_ref, inverse_ref, values_ref, shifted_ref, steps_ref[5], 0)
+    out_ref[...] = values_ref[3:11, :32]
+
+
+def post_smooth(steps, weights, edge, low, high, side, inverse, cells, below, beyond, left, right):
+    vmem = pl.BlockSpec(memory_space=pltpu.VMEM)
+    return pl.pallas_call(
+        post_kernel,
+        out_shape=jax.ShapeDtypeStruct((8, 32, 128), F32),
+        in_specs=[pl.BlockSpec(memory_space=pltpu.SMEM)] + [vmem] * 11,
+        scratch_shapes=stencil_scratch(),
+        compiler_params=pltpu.CompilerParams(vmem_limit_bytes=40 * 2**20),
+    )(steps, weights, edge, low, high, side, inverse, cells, below, beyond, left, right)
+
+
 SMOOTH = 3
 
 
-def extended_2(block, sides, width):
-    for axis, dim in sides:
-        count = lax.axis_size(axis)
-        forward = [(i, i + 1) for i in range(count - 1)]
-        backward = [(target, source) for source, target in forward]
-        low = lax.ppermute(
-            lax.slice_in_dim(block, block.shape[dim] - width, None, axis=dim), axis, forward
+def from_sides(axis, to_next, to_previous):
+    count = lax.axis_size(axis)
+    forward = [(i, i + 1) for i in range(count - 1)]
+    backward = [(target, source) for source, target in forward]
+    return lax.ppermute(to_next, axis, forward), lax.ppermute(to_previous, axis, backward)
+
+
+def halo_values(values):
+    low, high = from_sides("slab", values[5:], values[:3])
+
+    def rows(first):
+        return jnp.concatenate(
+            [low[:, first : first + 3], values[:, first : first + 3], high[:, first : first + 3]],
+            axis=0,
         )
-        high = lax.ppermute(lax.slice_in_dim(block, 0, width, axis=dim), axis, backward)
-        block = jnp.concatenate([low, block, high], axis=dim)
-    return block
-
-
-def apply_stencil(values, weights):
-    extended = extended_2(values, (("slab", 0), ("col", 1)), 1)
-    padded = jnp.pad(extended, ((0, 0), (0, 0), (1, 1)))
-    size_x, size_y, size_z = values.shape
-    summed = jnp.zeros_like(values)
-    for offset in range(27):
-        shift_x = offset // 9
-        shift_y = offset // 3 % 3
-        shift_z = offset % 3
-        summed = (
-            summed
-            + weights[offset]
-            * padded[
-                shift_x : shift_x + size_x, shift_y : shift_y + size_y, shift_z : shift_z + size_z
-            ]
-        )
-    return summed
-
-
-def sweeps(solution, right_side, weights, factors):
-    center = weights[13]
-    for sweep_index in range(factors.shape[0]):
-        residue = right_side - apply_stencil(solution, weights)
-        solution = solution + factors[sweep_index] * residue / center
-    return solution
+
+    left, right = from_sides("col", rows(29), rows(0))
+    return low, high, left, right
 
 
 def shards(
     right_side, stencil_weights, cheb_steps, send_slot, recv_index, coarse_diag, coarse_lower
 ):
-    slab_count = lax.axis_size("slab")
     me = lax.axis_index("slab")
-    cells_shape = right_side.shape
     diag, lower = coarse_diag[0, 0], coarse_lower[0, 0]
+    index = recv_index.reshape(64, 128)
     inverse = invert_one(diag[None])[0]
     mine = jnp.where(me % 2 == 1, inverse, diag)
-    every = lax.all_gather(jnp.concatenate([mine, lower])[None], "slab", axis=0, tiled=True)
-
-    table = lax.all_to_all(recv_index[0, 0], "slab", split_axis=0, concat_axis=0, tiled=True)
+    blocks = jnp.concatenate([mine, lower, index.astype(F32)])
+    every = lax.all_gather(blocks[None], "slab", axis=0, tiled=True)
+
+    to_next, to_previous, start = cut(stencil_weights, right_side)
+    left, right = from_sides("col", to_next, to_previous)
+    to_next, to_previous, edge, edge_start = pack(stencil_weights, right_side, start, left, right)
+    low, high = from_sides("slab", to_next, to_previous)
+    smooth, residue, side, inverse_center = pre_smooth(
+        cheb_steps, stencil_weights, edge, low, high, right_side, start, edge_start
+    )
     slot = send_slot.reshape(-1, 128)
-    unknown = lookup(slot, table.reshape(-1, 128))
-
-    smooth = cheb_steps[0] * right_side / stencil_weights[13]
-    smooth = sweeps(smooth, right_side, stencil_weights, cheb_steps[1:SMOOTH])
-    residue = right_side - apply_stencil(smooth, stencil_weights)
-    partial = scatter(slot, unknown, residue.reshape(-1, 128))
-    arrived = lax.all_to_all(partial, "slab", split_axis=0, concat_axis=0, tiled=True)
-    mine_rhs = jnp.sum(arrived, axis=0, keepdims=True)
-    rhs = lax.all_to_all(
-        jnp.broadcast_to(mine_rhs, arrived.shape), "slab", split_axis=0, concat_axis=0, tiled=True
+    sums = scatter(slot, residue.reshape(-1, 128)).reshape(32, 256)
+    arrived = lax.all_to_all(sums, "slab", split_axis=0, concat_axis=0, tiled=True)
+    mine_rhs = collect(index, arrived.reshape(64, 128))
+    rhs = lax.all_to_all(mine_rhs, "slab", split_axis=0, concat_axis=0, tiled=True)
+
+    table = lax.dynamic_slice_in_dim(every, 256 + 2 * me, 2, axis=1).reshape(64, 128)
+    unknown = lookup(slot, table)
+    coarse_x = solve(factor(every), rhs)
+    corrected = gather(slot, unknown, coarse_x, smooth.reshape(-1, 128)).reshape(right_side.shape)
+    return post_smooth(
+        cheb_steps, stencil_weights, edge, low, high, side, inverse_center,
+        corrected, *halo_values(corrected),
     )
-
-    factors = factor(every[:, :128], every[:, 128:])
-    coarse_x = solve(factors, rhs)
-    corrected = gather(slot, unknown, coarse_x, smooth.reshape(-1, 128)).reshape(cells_shape)
-    return sweeps(corrected, right_side, stencil_weights, cheb_steps[SMOOTH:])
 
 
 def solution(mesh):

time: 229 us -> 197 us (0.86); the launches traced: 225 us -> 196 us
  starting transfers between devices: 111 us -> 42 us
  waiting for transfers between devices: 7.92 us -> 56.5 us
  other arithmetic: 17.6 us -> 1.56 us
  Pallas kernels: 51.5 us -> 67.5 us
  blocking collectives: 13.5 us -> 0 us
  local copies, waits for them, and re-layouts: 9.18 us -> 14.7 us
    ppermute x24 -> x8, starting transfers between devices: 96.5 us -> 27.3 us  [the longest x4 19.6 us: from_sides(): lax.ppermute(to_next, axis, forward)]
    ppermute x24 -> x8, waiting for transfers between devices: 7.88 us -> 51.5 us  [the longest x4 29.3 us: from_sides(): lax.ppermute(to_next, axis, forward)]
    pallas_call x1 -> x6, Pallas kernels: 8.14 us -> 24.6 us  [the longest x1 8.81 us: scatter(): pl.pallas_call(scatter_kernel, out_shape=jax.ShapeDtypeStruct((64, 128),...]
    all_to_all x1 -> x0, blocking collectives: 13.5 us -> none  [shards(): lax.all_to_all(partial, 'slab', split_axis=0, concat_axis=0, tiled=True)]
    unnamed x14 -> x60, local copies, waits for them, and re-layouts: 3.65 us -> 13 us
    add x5 -> x0, other arithmetic: 9.32 us -> none  [sweeps(): solution = solution + factors[sweep_index] * residue / center]
    all_to_all x2, waiting for transfers between devices: 0.01 us -> 5.01 us  [the longest x1 5.01 us: shards(): lax.all_to_all(sums, 'slab', split_axis=0, concat_axis=0, tiled=True)]
    slice x8 -> x4, local copies, waits for them, and re-layouts: 4.29 us -> 0.03 us  [the longest x1 0.01 us: rows(): values[:, first:first + 3]]
  transfers between devices with their start and end apart: 27 -> 11, of which waited for: 10 -> 7; matrix products, arithmetic and copies ran while one was open for 7% -> 0% of each run, Pallas kernels for 18% -> 25%
where the time goes in v2:
time: 197 us; the launch traced here: 196 us
  Pallas kernels  67.5 us (34%)
  waiting for transfers between devices  56.5 us (29%)
  starting transfers between devices  42 us (21%)
  local copies, waits for them, and re-layouts  14.7 us (7%)
  between operations  13.8 us (7%)
    ppermute x4, waiting for transfers between devices, from_sides(): lax.ppermute(to_next, axis, forward)  29.3 us
    pallas_call x1, Pallas kernels, factor(): pl.pallas_call(functools.partial(factor_kernel, count), out_shape=jax.Sha...  24.8 us
    ppermute x4, waiting for transfers between devices, from_sides(): lax.ppermute(to_previous, axis, backward)  22.2 us
    ppermute x4, starting transfers between devices, from_sides(): lax.ppermute(to_next, axis, forward)  19.6 us
    unnamed x60, local copies, waits for them, and re-layouts  13 us
    pallas_call x1, Pallas kernels, scatter(): pl.pallas_call(scatter_kernel, out_shape=jax.ShapeDtypeStruct((64, 128),...  8.81 us
    all_to_all x1, starting transfers between devices, shards(): lax.all_to_all(mine_rhs, 'slab', split_axis=0, concat_axis=0, tiled=True)  7.76 us
    ppermute x4, starting transfers between devices, from_sides(): lax.ppermute(to_previous, axis, backward)  7.68 us
  transfers between devices with their start and end apart: 11, of which 7 were waited for; matrix products, arithmetic and copies ran while one was open for 0% of the time, Pallas kernels for 25%

profile of v2, /device:TPU:123, one launch (start us, length us, event | category | flops | bytes accessed | tf_op | source)
XLA Modules:
  0.0 196.0 jit_solution(10387713922643541703)
XLA Ops:
  8.2 1.3 shard_map.76
  9.5 1.5 pad_maximum_fusion
  11.1 2.0 %copy-done = f32[27,8,32,128]{3,2,1,0:T(8,128)S(1)} copy-done((f32[27,8,32,128]{3,2,1,0:T(8,128)S(1)}, f32[27,8,32,128]{3,2,1,0:T(8,128)}, u32[]{:S(2)}) %copy-start) | copy-done | bytes 3538968
  14.2 4.2 %collective-permute-start = (f32[240,2,128]{2,1,0:T(2,128)S(1)}, f32[240,2,128]{2,1,0:T(2,128)S(1)}, u32[]{:S(2)}, u32[]{:S(2)}) collective-permute-start(f32[240,2,128]{2,1,0:T(2,128)S(1)} %get-tuple-element.17), channel_id=1, source_target_pairs={{0,1},{1,2},{2,3},{3,4},{4,5},{5,6},{6,7},{8,9},{9,10},{10,11},{11... | collective-permute-start | bytes 737288 | tf_op jit(solution)/shard_map/ppermute | solution.py:503
  18.4 1.9 collective-permute-start.1
  20.3 1.2 collective-permute-done.left_ref
  21.5 4.4 %collective-permute-done.1.right_ref = f32[240,2,128]{2,1,0:T(2,128)S(1)} collective-permute-done((f32[240,2,128]{2,1,0:T(2,128)S(1)}, f32[240,2,128]{2,1,0:T(2,128)S(1)}, u32[]{:S(2)}, u32[]{:S(2)}) %collective-permute-start.1) | collective-permute-done | bytes 245792 | tf_op jit(solution)/shard_map/ppermute | solution.py:503
  25.9 1.7 shard_map.74
  27.6 4.4 %collective-permute-start.2 = (f32[59,40,128]{2,1,0:T(8,128)S(1)}, f32[59,40,128]{2,1,0:T(8,128)S(1)}, u32[]{:S(2)}, u32[]{:S(2)}) collective-permute-start(f32[59,40,128]{2,1,0:T(8,128)S(1)} %get-tuple-element.20), channel_id=1, source_target_pairs={{0,8},{8,16},{16,24},{24,32},{32,40},{40,48},{48,56},{56,64},{64,7... | collective-permute-start | bytes 3624968 | tf_op jit(solution)/shard_map/ppermute | solution.py:503
  32.0 1.9 collective-permute-start.3
  34.0 28.1 %collective-permute-done.2.low_ref = f32[59,40,128]{2,1,0:T(8,128)S(1)} collective-permute-done((f32[59,40,128]{2,1,0:T(8,128)S(1)}, f32[59,40,128]{2,1,0:T(8,128)S(1)}, u32[]{:S(2)}, u32[]{:S(2)}) %collective-permute-start.2) | collective-permute-done | bytes 1208352 | tf_op jit(solution)/shard_map/ppermute | solution.py:503
  62.1 8.3 %collective-permute-done.3.high_ref = f32[59,40,128]{2,1,0:T(8,128)S(1)} collective-permute-done((f32[59,40,128]{2,1,0:T(8,128)S(1)}, f32[59,40,128]{2,1,0:T(8,128)S(1)}, u32[]{:S(2)}, u32[]{:S(2)}) %collective-permute-start.3) | collective-permute-done | bytes 1208352 | tf_op jit(solution)/shard_map/ppermute | solution.py:503
  70.4 5.9 %shard_map.75 = (f32[8,32,128]{2,1,0:T(8,128)S(1)}, f32[8,32,128]{2,1,0:T(8,128)S(1)}, f32[12,40,128]{2,1,0:T(8,128)S(1)}, f32[12,40,128]{2,1,0:T(8,128)S(1)}) custom-call(f32[6]{0:T(128)S(1)} %copy-done.28, f32[27,8,32,128]{3,2,1,0:T(8,128)S(1)} %copy-done.1, f32[224,8,128]{2,1,0:T(8,128)S(1)} %get-tuple-element.19.edge_ref, ...), custom_call_target="tpu_custom_call" | custom-call | tf_op jit(solution)/shard_map/pallas_call | solution.py:455
  77.7 8.8 %shard_map.79 = f32[64,128]{1,0:T(8,128)S(1)} custom-call(s32[256,128]{1,0:T(8,128)S(1)} %bitcast.26, f32[256,128]{1,0:T(8,128)S(1)} %bitcast.32), custom_call_target="tpu_custom_call" | custom-call | tf_op jit(solution)/shard_map/pallas_call | solution.py:79
  87.1 6.9 %all-to-all-start = ((f32[32,1,256]{2,1,0:T(1,128)}), f32[32,1,256]{2,1,0:T(1,128)}, u32[]{:S(2)}, u32[]{:S(2)}) async-start(f32[32,1,256]{2,1,0:T(1,128)} %bitcast.30), calls=%async_computation | async-start | bytes 65536 | tf_op jit(solution)/shard_map/all_to_all | solution.py:539
  94.0 5.0 %all-to-all-done = f32[32,1,256]{2,1,0:T(1,128)} async-done(((f32[32,1,256]{2,1,0:T(1,128)}), f32[32,1,256]{2,1,0:T(1,128)}, u32[]{:S(2)}, u32[]{:S(2)}) %all-to-all-start) | async-done | bytes 32800 | tf_op jit(solution)/shard_map/all_to_all | solution.py:539
  99.8 1.4 shard_map.80
  101.8 7.8 %all-to-all-start.1 = ((f32[32,1,128]{2,1,0:T(1,128)}), f32[32,1,128]{2,1,0:T(1,128)S(1)}, u32[]{:S(2)}, u32[]{:S(2)}) async-start(f32[32,1,128]{2,1,0:T(1,128)} %bitcast.35), calls=%async_computation.1 | async-start | bytes 32768 | tf_op jit(solution)/shard_map/all_to_all | solution.py:541
  109.6 0.9 constant_dynamic-slice_fusion
  110.5 2.5 %copy-done.3 = f32[10240,128]{1,0:T(8,128)S(1)} copy-done((f32[10240,128]{1,0:T(8,128)S(1)}, f32[10240,128]{1,0:T(8,128)}, u32[]{:S(2)}) %copy-start.3) | copy-done | bytes 5242904
  113.0 24.8 %shard_map.78.factor_ref = f32[32,384,128]{2,1,0:T(8,128)} custom-call(f32[32,320,128]{2,1,0:T(8,128)S(1)} %bitcast.23), custom_call_target="tpu_custom_call" | custom-call | tf_op jit(solution)/shard_map/pallas_call | solution.py:249
  137.8 6.1 %shard_map.77.unknown_ref = s32[256,128]{1,0:T(8,128)S(1)} custom-call(s32[256,128]{1,0:T(8,128)S(1)} %bitcast.27, f32[64,128]{1,0:T(8,128)S(1)} %bitcast.31), custom_call_target="tpu_custom_call" | custom-call | tf_op jit(solution)/shard_map/pallas_call | solution.py:55
  144.6 2.8 %copy-done.2 = f32[32,384,128]{2,1,0:T(8,128)S(1)} copy-done((f32[32,384,128]{2,1,0:T(8,128)S(1)}, f32[32,384,128]{2,1,0:T(8,128)}, u32[]{:S(2)}) %copy-start.2) | copy-done | bytes 6291480
  147.4 4.6 %shard_map.81.table_ref = f32[32,128]{1,0:T(8,128)S(1)} custom-call(f32[32,384,128]{2,1,0:T(8,128)S(1)} %copy-done.2, f32[32,128]{1,0:T(8,128)S(1)} %bitcast.34), custom_call_target="tpu_custom_call" | custom-call | tf_op jit(solution)/shard_map/pallas_call | solution.py:287
  152.0 6.1 %shard_map.82 = f32[256,128]{1,0:T(8,128)S(1)} custom-call(s32[256,128]{1,0:T(8,128)S(1)} %bitcast.28, s32[256,128]{1,0:T(8,128)S(1)} %copy-done.16, f32[32,128]{1,0:T(8,128)S(1)} %shard_map.81.table_ref, f32[256,128]{1,0:T(8,128)S(1)} %bitcast.33), custom_call_target="tpu_custom_call" | custom-call | tf_op jit(solution)/shard_map/pallas_call | solution.py:115
  158.2 4.3 %collective-permute-start.4 = (f32[3,32,128]{2,1,0:T(8,128)S(1)}, f32[3,32,128]{2,1,0:T(8,128)S(1)}, u32[]{:S(2)}, u32[]{:S(2)}) collective-permute-start(f32[3,32,128]{2,1,0:T(8,128)S(1)} %bitcast.38), channel_id=1, source_target_pairs={{0,8},{8,16},{16,24},{24,32},{32,40},{40,48},{48,56},{56,64},{64,7... | collective-permute-start | bytes 147464 | tf_op jit(solution)/shard_map/ppermute | solution.py:503
  162.5 1.9 collective-permute-start.5
  164.5 6.2 %collective-permute-done.5.beyond_ref = f32[3,32,128]{2,1,0:T(8,128)S(1)} collective-permute-done((f32[3,32,128]{2,1,0:T(8,128)S(1)}, f32[3,32,128]{2,1,0:T(8,128)S(1)}, u32[]{:S(2)}, u32[]{:S(2)}) %collective-permute-start.5) | collective-permute-done | bytes 49184 | tf_op jit(solution)/shard_map/ppermute | solution.py:503
  170.7 6.7 %collective-permute-start.6 = (f32[14,3,128]{2,1,0:T(4,128)S(1)}, f32[14,3,128]{2,1,0:T(4,128)S(1)}, u32[]{:S(2)}, u32[]{:S(2)}) collective-permute-start(f32[14,3,128]{2,1,0:T(4,128)S(1)} %pad_maximum_fusion.1), channel_id=1, source_target_pairs={{0,1},{1,2},{2,3},{3,4},{4,5},{5,6},{6,7},{8,9},{9,10},{10,11},{11... | collective-permute-start | bytes 64520 | tf_op jit(solution)/shard_map/ppermute | solution.py:503
  177.4 1.9 collective-permute-start.7
  179.3 3.3 %collective-permute-done.7.right_ref = f32[14,3,128]{2,1,0:T(4,128)S(1)} collective-permute-done((f32[14,3,128]{2,1,0:T(4,128)S(1)}, f32[14,3,128]{2,1,0:T(4,128)S(1)}, u32[]{:S(2)}, u32[]{:S(2)}) %collective-permute-start.7) | collective-permute-done | bytes 21536 | tf_op jit(solution)/shard_map/ppermute | solution.py:503
  182.6 6.5 %shard_map.83 = f32[8,32,128]{2,1,0:T(8,128)} custom-call(f32[6]{0:T(128)S(1)} %copy-done.29, f32[27,8,32,128]{3,2,1,0:T(8,128)S(1)} %copy-done.1, f32[224,8,128]{2,1,0:T(8,128)S(1)} %copy-done.9, f32[59,40,128]{2,1,0:T(8,128)S(1)} %copy-done.5, f32[59,40,128]{2,1,0:T(8,128)S(1)} %copy-done.7, f32[12,40,128]{2,1,0:T(8,128)S(1)} %copy-done.21, ...), custom_call_target="tpu_custom_call" | custom-call | tf_op jit(solution)/shard_map/pallas_call | solution.py:487
  (73 shorter events, 6.8 us)
Async XLA Ops:
  6.5 103.0 %all-gather.3.cloned.1.call-start = ((), (), s32[]{:S(2)}) async-start(), calls=%async_computation.2 | async-start | bytes 5406720 | tf_op jit(solution)/shard_map/all_gather | solution.py:528
  7.3 3.7 %copy-start.17 = (s32[64,128]{1,0:T(8,128)}, s32[64,128]{1,0:T(8,128)S(1)}, u32[]{:S(2)}) copy-start(s32[64,128]{1,0:T(8,128)S(1)} %reshape.31.index_ref) | copy-start | bytes 98308
  14.0 11.9 %copy-start.1 = (f32[27,8,32,128]{3,2,1,0:T(8,128)S(1)}, f32[27,8,32,128]{3,2,1,0:T(8,128)}, u32[]{:S(2)}) copy-start(f32[27,8,32,128]{3,2,1,0:T(8,128)} %main_ref.3) | copy-start | bytes 10616836
  14.0 11.9 %copy-start.11 = (f32[8,32,128]{2,1,0:T(8,128)S(1)}, f32[8,32,128]{2,1,0:T(8,128)}, u32[]{:S(2)}) copy-start(f32[8,32,128]{2,1,0:T(8,128)} %side_main_ref.1) | copy-start | bytes 393220
  14.0 56.4 %copy-start.28 = (f32[6]{0:T(128)S(1)}, f32[6]{0:T(128)}, u32[]{:S(2)}) copy-start(f32[6]{0:T(128)} %steps_ref.3) | copy-start | bytes 76
  14.2 7.4 %collective-permute-start = (f32[240,2,128]{2,1,0:T(2,128)S(1)}, f32[240,2,128]{2,1,0:T(2,128)S(1)}, u32[]{:S(2)}, u32[]{:S(2)}) collective-permute-start(f32[240,2,128]{2,1,0:T(2,128)S(1)} %get-tuple-element.17), channel_id=1, source_target_pairs={{0,1},{1,2},{2,3},{3,4},{4,5},{5,6},{6,7},{8,9},{9,10},{10,11},{11... | collective-permute-start | bytes 737288 | tf_op jit(solution)/shard_map/ppermute | solution.py:503
  18.4 7.5 %collective-permute-start.1 = (f32[240,2,128]{2,1,0:T(2,128)S(1)}, f32[240,2,128]{2,1,0:T(2,128)S(1)}, u32[]{:S(2)}, u32[]{:S(2)}) collective-permute-start(f32[240,2,128]{2,1,0:T(2,128)S(1)} %get-tuple-element.18), channel_id=1, source_target_pairs={{1,0},{2,1},{3,2},{4,3},{5,4},{6,5},{7,6},{9,8},{10,9},{11,10},{12... | collective-permute-start | bytes 737288 | tf_op jit(solution)/shard_map/ppermute | solution.py:503
  27.6 48.7 %copy-start.8 = (f32[224,8,128]{2,1,0:T(8,128)}, f32[224,8,128]{2,1,0:T(8,128)S(1)}, u32[]{:S(2)}) copy-start(f32[224,8,128]{2,1,0:T(8,128)S(1)} %get-tuple-element.19.edge_ref) | copy-start | bytes 2752516
  27.6 34.4 %collective-permute-start.2 = (f32[59,40,128]{2,1,0:T(8,128)S(1)}, f32[59,40,128]{2,1,0:T(8,128)S(1)}, u32[]{:S(2)}, u32[]{:S(2)}) collective-permute-start(f32[59,40,128]{2,1,0:T(8,128)S(1)} %get-tuple-element.20), channel_id=1, source_target_pairs={{0,8},{8,16},{16,24},{24,32},{32,40},{40,48},{48,56},{56,64},{64,7... | collective-permute-start | bytes 3624968 | tf_op jit(solution)/shard_map/ppermute | solution.py:503
  32.0 38.3 %collective-permute-start.3 = (f32[59,40,128]{2,1,0:T(8,128)S(1)}, f32[59,40,128]{2,1,0:T(8,128)S(1)}, u32[]{:S(2)}, u32[]{:S(2)}) collective-permute-start(f32[59,40,128]{2,1,0:T(8,128)S(1)} %get-tuple-element.21), channel_id=1, source_target_pairs={{8,0},{16,8},{24,16},{32,24},{40,32},{48,40},{56,48},{64,56},{72,6... | collective-permute-start | bytes 3624968 | tf_op jit(solution)/shard_map/ppermute | solution.py:503
  62.1 14.3 %copy-start.4 = (f32[59,40,128]{2,1,0:T(8,128)}, f32[59,40,128]{2,1,0:T(8,128)S(1)}, u32[]{:S(2)}) copy-start(f32[59,40,128]{2,1,0:T(8,128)S(1)} %collective-permute-done.2.low_ref) | copy-start | bytes 3624964
  70.4 6.0 %copy-start.6 = (f32[59,40,128]{2,1,0:T(8,128)}, f32[59,40,128]{2,1,0:T(8,128)S(1)}, u32[]{:S(2)}) copy-start(f32[59,40,128]{2,1,0:T(8,128)S(1)} %collective-permute-done.3.high_ref) | copy-start | bytes 3624964
  70.4 7.3 %copy-start.12 = (s32[8,32,128]{2,1,0:T(8,128)S(1)}, s32[8,32,128]{2,1,0:T(8,128)}, u32[]{:S(2)}) copy-start(s32[8,32,128]{2,1,0:T(8,128)} %param.10) | copy-start | bytes 393220
  77.7 8.8 %copy-start.20 = (f32[12,40,128]{2,1,0:T(8,128)}, f32[12,40,128]{2,1,0:T(8,128)S(1)}, u32[]{:S(2)}) copy-start(f32[12,40,128]{2,1,0:T(8,128)S(1)} %get-tuple-element.23.side_ref) | copy-start | bytes 737284
  87.1 11.9 %all-to-all-start = ((f32[32,1,256]{2,1,0:T(1,128)}), f32[32,1,256]{2,1,0:T(1,128)}, u32[]{:S(2)}, u32[]{:S(2)}) async-start(f32[32,1,256]{2,1,0:T(1,128)} %bitcast.30), calls=%async_computation | async-start | bytes 65536 | tf_op jit(solution)/shard_map/all_to_all | solution.py:539
  101.8 42.8 %all-to-all-start.1 = ((f32[32,1,128]{2,1,0:T(1,128)}), f32[32,1,128]{2,1,0:T(1,128)S(1)}, u32[]{:S(2)}, u32[]{:S(2)}) async-start(f32[32,1,128]{2,1,0:T(1,128)} %bitcast.35), calls=%async_computation.1 | async-start | bytes 32768 | tf_op jit(solution)/shard_map/all_to_all | solution.py:541
  110.5 2.5 %copy-start.3 = (f32[10240,128]{1,0:T(8,128)S(1)}, f32[10240,128]{1,0:T(8,128)}, u32[]{:S(2)}) copy-start(f32[10240,128]{1,0:T(8,128)} %all-gather.3.cloned.1.call-done) | copy-start | bytes 15728644
  113.0 24.8 %copy-start.13 = (s32[8,32,128]{2,1,0:T(8,128)S(1)}, s32[8,32,128]{2,1,0:T(8,128)}, u32[]{:S(2)}) copy-start(s32[8,32,128]{2,1,0:T(8,128)} %param.10) | copy-start | bytes 393220
  144.6 2.8 %copy-start.2 = (f32[32,384,128]{2,1,0:T(8,128)S(1)}, f32[32,384,128]{2,1,0:T(8,128)}, u32[]{:S(2)}) copy-start(f32[32,384,128]{2,1,0:T(8,128)} %shard_map.78.factor_ref) | copy-start | bytes 18874372
  147.4 4.6 %copy-start.14 = (s32[8,32,128]{2,1,0:T(8,128)S(1)}, s32[8,32,128]{2,1,0:T(8,128)}, u32[]{:S(2)}) copy-start(s32[8,32,128]{2,1,0:T(8,128)} %param.10) | copy-start | bytes 393220
  147.4 4.6 %copy-start.16 = (s32[256,128]{1,0:T(8,128)S(1)}, s32[256,128]{1,0:T(8,128)}, u32[]{:S(2)}) copy-start(s32[256,128]{1,0:T(8,128)} %copy-done.15) | copy-start | bytes 393220
  147.4 4.6 %copy-start.26 = (f32[8,32,128]{2,1,0:T(8,128)S(1)}, f32[8,32,128]{2,1,0:T(8,128)}, u32[]{:S(2)}) copy-start(f32[8,32,128]{2,1,0:T(8,128)} %copy-done.25) | copy-start | bytes 393220
  147.4 35.2 %copy-start.5 = (f32[59,40,128]{2,1,0:T(8,128)S(1)}, f32[59,40,128]{2,1,0:T(8,128)}, u32[]{:S(2)}) copy-start(f32[59,40,128]{2,1,0:T(8,128)} %copy-done.4) | copy-start | bytes 3624964
  147.4 35.2 %copy-start.7 = (f32[59,40,128]{2,1,0:T(8,128)S(1)}, f32[59,40,128]{2,1,0:T(8,128)}, u32[]{:S(2)}) copy-start(f32[59,40,128]{2,1,0:T(8,128)} %copy-done.6) | copy-start | bytes 3624964
  147.4 35.2 %copy-start.9 = (f32[224,8,128]{2,1,0:T(8,128)S(1)}, f32[224,8,128]{2,1,0:T(8,128)}, u32[]{:S(2)}) copy-start(f32[224,8,128]{2,1,0:T(8,128)} %copy-done.8) | copy-start | bytes 2752516
  147.4 35.2 %copy-start.21 = (f32[12,40,128]{2,1,0:T(8,128)S(1)}, f32[12,40,128]{2,1,0:T(8,128)}, u32[]{:S(2)}) copy-start(f32[12,40,128]{2,1,0:T(8,128)} %copy-done.20) | copy-start | bytes 737284
  147.4 35.2 %copy-start.23 = (f32[12,40,128]{2,1,0:T(8,128)S(1)}, f32[12,40,128]{2,1,0:T(8,128)}, u32[]{:S(2)}) copy-start(f32[12,40,128]{2,1,0:T(8,128)} %copy-done.22) | copy-start | bytes 737284
  147.4 35.2 %copy-start.29 = (f32[6]{0:T(128)S(1)}, f32[6]{0:T(128)}, u32[]{:S(2)}) copy-start(f32[6]{0:T(128)} %steps_ref.3) | copy-start | bytes 76
  158.2 6.3 %collective-permute-start.4 = (f32[3,32,128]{2,1,0:T(8,128)S(1)}, f32[3,32,128]{2,1,0:T(8,128)S(1)}, u32[]{:S(2)}, u32[]{:S(2)}) collective-permute-start(f32[3,32,128]{2,1,0:T(8,128)S(1)} %bitcast.38), channel_id=1, source_target_pairs={{0,8},{8,16},{16,24},{24,32},{32,40},{40,48},{48,56},{56,64},{64,7... | collective-permute-start | bytes 147464 | tf_op jit(solution)/shard_map/ppermute | solution.py:503
  162.5 8.2 %collective-permute-start.5 = (f32[3,32,128]{2,1,0:T(8,128)S(1)}, f32[3,32,128]{2,1,0:T(8,128)S(1)}, u32[]{:S(2)}, u32[]{:S(2)}) collective-permute-start(f32[3,32,128]{2,1,0:T(8,128)S(1)} %bitcast.37), channel_id=1, source_target_pairs={{8,0},{16,8},{24,16},{32,24},{40,32},{48,40},{56,48},{64,56},{72,6... | collective-permute-start | bytes 147464 | tf_op jit(solution)/shard_map/ppermute | solution.py:503
  170.7 8.7 %collective-permute-start.6 = (f32[14,3,128]{2,1,0:T(4,128)S(1)}, f32[14,3,128]{2,1,0:T(4,128)S(1)}, u32[]{:S(2)}, u32[]{:S(2)}) collective-permute-start(f32[14,3,128]{2,1,0:T(4,128)S(1)} %pad_maximum_fusion.1), channel_id=1, source_target_pairs={{0,1},{1,2},{2,3},{3,4},{4,5},{5,6},{6,7},{8,9},{9,10},{10,11},{11... | collective-permute-start | bytes 64520 | tf_op jit(solution)/shard_map/ppermute | solution.py:503
  177.4 5.2 %collective-permute-start.7 = (f32[14,3,128]{2,1,0:T(4,128)S(1)}, f32[14,3,128]{2,1,0:T(4,128)S(1)}, u32[]{:S(2)}, u32[]{:S(2)}) collective-permute-start(f32[14,3,128]{2,1,0:T(4,128)S(1)} %pad_maximum_fusion.2), channel_id=1, source_target_pairs={{1,0},{2,1},{3,2},{4,3},{5,4},{6,5},{7,6},{9,8},{10,9},{11,10},{12... | collective-permute-start | bytes 64520 | tf_op jit(solution)/shard_map/ppermute | solution.py:503
  (9 other events, 7.7 us)
Sparse Core Ops, SparseCore 0:
  11.2 84.9 all-gather.2

commit v3 on v2

--- a/solution.py
+++ b/solution.py
@@ -10,6 +10,7 @@
 F32 = jnp.float32
 BF16 = jnp.bfloat16
 ROWS = 40
+SMOOTH = 3
 
 
 def nn(a, b):
@@ -24,7 +25,9 @@
 
 def one_hot(index_row, size):
     width = index_row.shape[1]
-    return (lax.broadcasted_iota(jnp.int32, (size, width), 0) == index_row).astype(F32).astype(BF16)
+    wide = jnp.broadcast_to(index_row.astype(F32), (size, width)).astype(BF16)
+    rows = lax.broadcasted_iota(jnp.int32, (size, width), 0).astype(F32).astype(BF16)
+    return jnp.where(rows == wide, jnp.bfloat16(1), jnp.bfloat16(0))
 
 def pair(block, first):
     return jnp.concatenate([block[first : first + 1], block[first + 1 : first + 2]], axis=1)
@@ -41,55 +44,64 @@
         rows += [row[:, :128], row[:, 128:]]
     return jnp.concatenate(rows, axis=0)
 
+def slot_row(slot):
+    return ((slot >> 7) & 1) * 32 + (slot >> 8)
+
+
 def lookup_kernel(slot_ref, table_ref, out_ref):
     table = table_ref[...].astype(BF16)
 
-    @pl.loop(0, slot_ref.shape[0] // 8)
+    @pl.loop(0, slot_ref.shape[0] // 8, unroll=8)
     def _(block):
         where = pl.ds(pl.multiple_of(block * 8, 8), 8)
         slot = slot_ref[where]
-        found = gather_rows(table, 64, 1, slot >> 7, slot & 127)
+        found = gather_rows(table, 64, 1, slot_row(slot), slot & 127)
         out_ref[where] = found.astype(jnp.int32)
+
 
 def lookup(slot, table):
     return pl.pallas_call(
         lookup_kernel,
         out_shape=jax.ShapeDtypeStruct(slot.shape, jnp.int32),
-        compiler_params=pltpu.CompilerParams(vmem_limit_bytes=16 * 2**20),
+        compiler_params=pltpu.CompilerParams(vmem_limit_bytes=8 * 2**20),
     )(slot, table)
+
 
 def scatter_kernel(slot_ref, value_ref, out_ref):
     def step(block, total):
         where = pl.ds(pl.multiple_of(block * 8, 8), 8)
         slot = slot_ref[where]
-        high_slot, low_slot = slot >> 7, slot & 127
+        high_slot, low_slot = slot_row(slot), slot & 127
         value = value_ref[where]
+        value_high = value.astype(BF16).astype(F32)
+        value_low = value - value_high
         for first in range(0, 8, 2):
             mask = lax.broadcasted_iota(jnp.int32, (64, 256), 0) == pair(high_slot, first)
-            spread = jnp.where(mask, pair(value, first), 0.0)
-            high, low = split(spread)
+            high = jnp.where(mask, pair(value_high, first), 0.0).astype(BF16)
+            low = jnp.where(mask, pair(value_low, first), 0.0).astype(BF16)
             total = total + nt(jnp.concatenate([high, low], axis=0), one_hot(pair(low_slot, first), 128))
         return total
 
-    total = lax.fori_loop(0, slot_ref.shape[0] // 8, step, jnp.zeros((128, 128), F32))
-    out_ref[...] = total[:64] + total[64:]
+    total = lax.fori_loop(0, slot_ref.shape[0] // 8, step, jnp.zeros((128, 128), F32), unroll=8)
+    total = total[:64] + total[64:]
+    out_ref[...] = jnp.concatenate([total[:32], total[32:]], axis=1)
 
 
 def scatter(slot, value):
     return pl.pallas_call(
         scatter_kernel,
-        out_shape=jax.ShapeDtypeStruct((64, 128), F32),
-        compiler_params=pltpu.CompilerParams(vmem_limit_bytes=16 * 2**20),
+        out_shape=jax.ShapeDtypeStruct((32, 256), F32),
+        compiler_params=pltpu.CompilerParams(vmem_limit_bytes=8 * 2**20),
     )(slot, value)
 
 
 def collect_kernel(index_ref, value_ref, out_ref):
     total = jnp.zeros((16, 128), F32)
-    for first in range(0, 64, 2):
-        row = pair(value_ref[...], first)
+    for source in range(32):
+        row = value_ref[source : source + 1]
         high, low = split(jnp.concatenate([row] * 8, axis=0))
         spread = jnp.concatenate([high, low], axis=0)
-        total = total + nt(spread, one_hot(pair(index_ref[...], first), 128))
+        total = total + nt(spread, one_hot(index_ref[source : source + 1], 128))
     row = total[0:1] + total[8:9]
     out_ref[...] = jnp.concatenate([row] * 32, axis=0)
 
@@ -98,7 +110,7 @@
     return pl.pallas_call(
         collect_kernel,
         out_shape=jax.ShapeDtypeStruct((32, 128), F32),
-        compiler_params=pltpu.CompilerParams(vmem_limit_bytes=16 * 2**20),
+        compiler_params=pltpu.CompilerParams(vmem_limit_bytes=8 * 2**20),
     )(index, value)
 
 
@@ -106,16 +118,19 @@
     high, low = split(table_ref[...])
     table = jnp.concatenate([high, low], axis=0)
 
-    @pl.loop(0, slot_ref.shape[0] // 8)
+    @pl.loop(0, slot_ref.shape[0] // 8, unroll=8)
     def _(block):
         where = pl.ds(pl.multiple_of(block * 8, 8), 8)
-        out_ref[where] = base_ref[where] + gather_rows(table, 32, 2, slot_ref[where] >> 8, unknown_ref[where])
+        rows = pl.ds(pl.multiple_of((block % 4) * 8, 8), 8)
+        found = gather_rows(table, 32, 2, slot_ref[where] >> 8, unknown_ref[where])
+        out_ref[block // 4, rows] = base_ref[block // 4, rows] + found
+
 
 def gather(slot, unknown, table, base):
     return pl.pallas_call(
         gather_kernel,
         out_shape=jax.ShapeDtypeStruct(base.shape, F32),
-        compiler_params=pltpu.CompilerParams(vmem_limit_bytes=16 * 2**20),
+        compiler_params=pltpu.CompilerParams(vmem_limit_bytes=8 * 2**20),
     )(slot, unknown, table, base)
 
 
@@ -201,16 +216,25 @@
     lax.while_loop(newton_cond, newton, (first, jnp.int32(0)))
     correct()
 
-def invert_kernel(a_ref, x_ref, r_ref):
-    invert(1, lambda b: a_ref[b], x_ref, r_ref)
-
-def invert_one(a):
-    return pl.pallas_call(
-        invert_kernel,
-        out_shape=jax.ShapeDtypeStruct((1, 128, 128), F32),
-        scratch_shapes=[pltpu.VMEM((1, 128, 128), F32)],
-        compiler_params=pltpu.CompilerParams(vmem_limit_bytes=16 * 2**20),
-    )(a)
+def blocks_kernel(place_ref, diag_ref, lower_ref, index_ref, out_ref, x_ref, r_ref):
+    invert(1, lambda b: diag_ref[...], x_ref, r_ref)
+    odd = place_ref[0] % 2 == 1
+    out_ref[0:128] = jnp.where(odd, x_ref[0], diag_ref[...])
+    out_ref[128:256] = lower_ref[...]
+    out_ref[256:288] = index_ref[:, :128].astype(F32)
+    out_ref[288:320] = index_ref[:, 128:].astype(F32)
+
+
+def own_blocks(place, diag, lower, index):
+    vmem = pl.BlockSpec(memory_space=pltpu.VMEM)
+    return pl.pallas_call(
+        blocks_kernel,
+        out_shape=jax.ShapeDtypeStruct((320, 128), F32),
+        in_specs=[pl.BlockSpec(memory_space=pltpu.SMEM), vmem, vmem, vmem],
+        scratch_shapes=[pltpu.VMEM((1, 128, 128), F32), pltpu.VMEM((1, 128, 128), F32)],
+        compiler_params=pltpu.CompilerParams(vmem_limit_bytes=4 * 2**20),
+    )(place, diag, lower, index)
+
 
 def factor_kernel(count, every_ref, out_ref, d_ref, l_ref, x_ref, r_ref):
     diag_ref = every_ref.at[:, 0:128]
@@ -255,8 +279,9 @@
             pltpu.VMEM((count // 4, 128, 128), F32),
             pltpu.VMEM((count // 4, 128, 128), F32),
         ],
-        compiler_params=pltpu.CompilerParams(vmem_limit_bytes=48 * 2**20),
+        compiler_params=pltpu.CompilerParams(vmem_limit_bytes=22 * 2**20),
     )(every)
+
 
 def solve_kernel(count, factor_ref, rhs_ref, out_ref, r_ref):
     def row3(form, row, mat):
@@ -288,7 +313,7 @@
         functools.partial(solve_kernel, count),
         out_shape=jax.ShapeDtypeStruct((count, 128), F32),
         scratch_shapes=[pltpu.VMEM((count, 128), F32)],
-        compiler_params=pltpu.CompilerParams(vmem_limit_bytes=32 * 2**20),
+        compiler_params=pltpu.CompilerParams(vmem_limit_bytes=10 * 2**20),
     )(factors, rhs)
 
 
@@ -312,7 +337,7 @@
     return pl.pallas_call(
         cut_kernel,
         out_shape=(rows, rows, jax.ShapeDtypeStruct((8, 32, 128), F32)),
-        compiler_params=pltpu.CompilerParams(vmem_limit_bytes=32 * 2**20),
+        compiler_params=pltpu.CompilerParams(vmem_limit_bytes=10 * 2**20),
     )(weights, side)
 
 
@@ -362,14 +387,14 @@
             planes, planes,
             jax.ShapeDtypeStruct((224, 8, 128), F32), jax.ShapeDtypeStruct((8, 8, 128), F32),
         ),
-        compiler_params=pltpu.CompilerParams(vmem_limit_bytes=40 * 2**20),
+        compiler_params=pltpu.CompilerParams(vmem_limit_bytes=16 * 2**20),
     )(weights, side, start, left, right)
 
 
 def shifted_planes(values_ref, shifted_ref, first, count):
     lane = lax.broadcasted_iota(jnp.int32, (ROWS, 128), 1)
 
-    @pl.loop(first, first + count)
+    @pl.loop(first, first + count, unroll=2)
     def _(x):
         plane = values_ref[x]
         below = jnp.where(lane == 0, 0.0, pltpu.roll(plane, 1, 1))
@@ -403,7 +428,7 @@
     for x in range(10, 10 + reach):
         update(lambda o: high_ref[2 * o + x - 10], x, 0, ROWS)
 
-    @pl.loop(0, 8)
+    @pl.loop(0, 8, unroll=2)
     def _(x):
         update(lambda o: main_ref[o, x], x + 2, 0, 32)
         if reach:
@@ -457,7 +482,7 @@
         out_shape=(cells, cells, outside, outside),
         in_specs=[pl.BlockSpec(memory_space=pltpu.SMEM)] + [vmem] * 7,
         scratch_shapes=stencil_scratch(),
-        compiler_params=pltpu.CompilerParams(vmem_limit_bytes=40 * 2**20),
+        compiler_params=pltpu.CompilerParams(vmem_limit_bytes=16 * 2**20),
     )(steps, weights, edge, low, high, side, start, edge_start)
 
 
@@ -489,11 +514,8 @@
         out_shape=jax.ShapeDtypeStruct((8, 32, 128), F32),
         in_specs=[pl.BlockSpec(memory_space=pltpu.SMEM)] + [vmem] * 11,
         scratch_shapes=stencil_scratch(),
-        compiler_params=pltpu.CompilerParams(vmem_limit_bytes=40 * 2**20),
+        compiler_params=pltpu.CompilerParams(vmem_limit_bytes=16 * 2**20),
     )(steps, weights, edge, low, high, side, inverse, cells, below, beyond, left, right)
-
-
-SMOOTH = 3
 
 
 def from_sides(axis, to_next, to_previous):
@@ -520,11 +542,9 @@
     right_side, stencil_weights, cheb_steps, send_slot, recv_index, coarse_diag, coarse_lower
 ):
     me = lax.axis_index("slab")
-    diag, lower = coarse_diag[0, 0], coarse_lower[0, 0]
-    index = recv_index.reshape(64, 128)
-    inverse = invert_one(diag[None])[0]
-    mine = jnp.where(me % 2 == 1, inverse, diag)
-    blocks = jnp.concatenate([mine, lower, index.astype(F32)])
+    index = recv_index[0, 0]
+    place = jnp.reshape(me, (1,)).astype(jnp.int32)
+    blocks = own_blocks(place, coarse_diag[0, 0], coarse_lower[0, 0], index)
     every = lax.all_gather(blocks[None], "slab", axis=0, tiled=True)
 
     to_next, to_previous, start = cut(stencil_weights, right_side)
@@ -535,15 +555,20 @@
         cheb_steps, stencil_weights, edge, low, high, right_side, start, edge_start
     )
     slot = send_slot.reshape(-1, 128)
-    sums = scatter(slot, residue.reshape(-1, 128)).reshape(32, 256)
+    sums = scatter(slot, residue.reshape(-1, 128))
     arrived = lax.all_to_all(sums, "slab", split_axis=0, concat_axis=0, tiled=True)
-    mine_rhs = collect(index, arrived.reshape(64, 128))
+    mine_rhs = collect(index, arrived)
     rhs = lax.all_to_all(mine_rhs, "slab", split_axis=0, concat_axis=0, tiled=True)
 
-    table = lax.dynamic_slice_in_dim(every, 256 + 2 * me, 2, axis=1).reshape(64, 128)
+    table = jnp.concatenate(
+        [
+            lax.dynamic_index_in_dim(every, 256 + me, 1, False),
+            lax.dynamic_index_in_dim(every, 288 + me, 1, False),
+        ]
+    )
     unknown = lookup(slot, table)
     coarse_x = solve(factor(every), rhs)
-    corrected = gather(slot, unknown, coarse_x, smooth.reshape(-1, 128)).reshape(right_side.shape)
+    corrected = gather(slot, unknown, coarse_x, smooth)
     return post_smooth(
         cheb_steps, stencil_weights, edge, low, high, side, inverse_center,
         corrected, *halo_values(corrected),

time: 197 us -> 181 us (0.919)
  the two profiles are of different devices: /device:TPU:123 before, /device:TPU:33 now
where the time goes in v3:
time: 181 us; the launch traced here: 180 us
  waiting for transfers between devices  50 us (28%)
  Pallas kernels  48.6 us (27%)
  starting transfers between devices  48.5 us (27%)
  local copies, waits for them, and re-layouts  19.2 us (11%)
  between operations  13.8 us (8%)
    ppermute x4, waiting for transfers between devices, from_sides(): lax.ppermute(to_next, axis, forward)  33.6 us
    pallas_call x1, Pallas kernels, factor(): pl.pallas_call(functools.partial(factor_kernel, count), out_shape=jax.Sha...  22.5 us
    ppermute x4, starting transfers between devices, from_sides(): lax.ppermute(to_next, axis, forward)  20.1 us
    unnamed x63, local copies, waits for them, and re-layouts  17.5 us
    ppermute x4, starting transfers between devices, from_sides(): lax.ppermute(to_previous, axis, backward)  12.3 us
    all_to_all x1, starting transfers between devices, shards(): lax.all_to_all(sums, 'slab', split_axis=0, concat_axis=0, tiled=True)  11.5 us
    ppermute x4, waiting for transfers between devices, from_sides(): lax.ppermute(to_previous, axis, backward)  8.37 us
    all_to_all x1, waiting for transfers between devices, shards(): lax.all_to_all(sums, 'slab', split_axis=0, concat_axis=0, tiled=True)  7.96 us
  transfers between devices with their start and end apart: 11, of which 7 were waited for; matrix products, arithmetic and copies ran while one was open for 1% of the time, Pallas kernels for 19%

profile of v3, /device:TPU:33, one launch (start us, length us, event | category | flops | bytes accessed | tf_op | source)
XLA Modules:
  0.0 180.2 jit_solution(492867931363490793)
XLA Ops:
  7.3 0.8 copy-done.26
  9.0 2.3 %shard_map.76 = f32[320,128]{1,0:T(8,128)} custom-call(s32[1]{0:T(128)} %bitcast.1.place_ref, f32[128,128]{1,0:T(8,128)S(1)} %bitcast.28, f32[128,128]{1,0:T(8,128)S(1)} %bitcast.29, s32[32,256]{1,0:T(8,128)S(1)} %bitcast.22), custom_call_target="tpu_custom_call" | custom-call | tf_op jit(solution)/shard_map/pallas_call | solution.py:230
  11.3 2.0 %copy-done = f32[27,8,32,128]{3,2,1,0:T(8,128)S(1)} copy-done((f32[27,8,32,128]{3,2,1,0:T(8,128)S(1)}, f32[27,8,32,128]{3,2,1,0:T(8,128)}, u32[]{:S(2)}) %copy-start) | copy-done | bytes 3538968
  13.3 0.9 copy-done.11
  14.4 3.7 %collective-permute-start = (f32[240,2,128]{2,1,0:T(2,128)S(1)}, f32[240,2,128]{2,1,0:T(2,128)S(1)}, u32[]{:S(2)}, u32[]{:S(2)}) collective-permute-start(f32[240,2,128]{2,1,0:T(2,128)S(1)} %get-tuple-element.17), channel_id=1, source_target_pairs={{0,1},{1,2},{2,3},{3,4},{4,5},{5,6},{6,7},{8,9},{9,10},{10,11},{11... | collective-permute-start | bytes 737288 | tf_op jit(solution)/shard_map/ppermute | solution.py:525
  18.1 1.9 %collective-permute-start.1 = (f32[240,2,128]{2,1,0:T(2,128)S(1)}, f32[240,2,128]{2,1,0:T(2,128)S(1)}, u32[]{:S(2)}, u32[]{:S(2)}) collective-permute-start(f32[240,2,128]{2,1,0:T(2,128)S(1)} %get-tuple-element.18), channel_id=1, source_target_pairs={{1,0},{2,1},{3,2},{4,3},{5,4},{6,5},{7,6},{9,8},{10,9},{11,10},{12... | collective-permute-start | bytes 737288 | tf_op jit(solution)/shard_map/ppermute | solution.py:525
  20.0 1.2 collective-permute-done.left_ref
  21.2 4.4 %collective-permute-done.1.right_ref = f32[240,2,128]{2,1,0:T(2,128)S(1)} collective-permute-done((f32[240,2,128]{2,1,0:T(2,128)S(1)}, f32[240,2,128]{2,1,0:T(2,128)S(1)}, u32[]{:S(2)}, u32[]{:S(2)}) %collective-permute-start.1) | collective-permute-done | bytes 245792 | tf_op jit(solution)/shard_map/ppermute | solution.py:525
  25.6 1.7 shard_map.74
  27.3 3.2 %collective-permute-start.2 = (f32[59,40,128]{2,1,0:T(8,128)S(1)}, f32[59,40,128]{2,1,0:T(8,128)S(1)}, u32[]{:S(2)}, u32[]{:S(2)}) collective-permute-start(f32[59,40,128]{2,1,0:T(8,128)S(1)} %get-tuple-element.20), channel_id=1, source_target_pairs={{0,8},{8,16},{16,24},{24,32},{32,40},{40,48},{48,56},{56,64},{64,7... | collective-permute-start | bytes 3624968 | tf_op jit(solution)/shard_map/ppermute | solution.py:525
  30.5 4.2 %collective-permute-start.3 = (f32[59,40,128]{2,1,0:T(8,128)S(1)}, f32[59,40,128]{2,1,0:T(8,128)S(1)}, u32[]{:S(2)}, u32[]{:S(2)}) collective-permute-start(f32[59,40,128]{2,1,0:T(8,128)S(1)} %get-tuple-element.21), channel_id=1, source_target_pairs={{8,0},{16,8},{24,16},{32,24},{40,32},{48,40},{56,48},{64,56},{72,6... | collective-permute-start | bytes 3624968 | tf_op jit(solution)/shard_map/ppermute | solution.py:525
  34.7 27.5 %collective-permute-done.2.low_ref = f32[59,40,128]{2,1,0:T(8,128)S(1)} collective-permute-done((f32[59,40,128]{2,1,0:T(8,128)S(1)}, f32[59,40,128]{2,1,0:T(8,128)S(1)}, u32[]{:S(2)}, u32[]{:S(2)}) %collective-permute-start.2) | collective-permute-done | bytes 1208352 | tf_op jit(solution)/shard_map/ppermute | solution.py:525
  62.9 4.5 %shard_map.75 = (f32[8,32,128]{2,1,0:T(8,128)S(1)}, f32[8,32,128]{2,1,0:T(8,128)S(1)}, f32[12,40,128]{2,1,0:T(8,128)S(1)}, f32[12,40,128]{2,1,0:T(8,128)S(1)}) custom-call(f32[6]{0:T(128)S(1)} %copy-done.29, f32[27,8,32,128]{3,2,1,0:T(8,128)S(1)} %copy-done.1, f32[224,8,128]{2,1,0:T(8,128)S(1)} %get-tuple-element.19.edge_ref, ...), custom_call_target="tpu_custom_call" | custom-call | tf_op jit(solution)/shard_map/pallas_call | solution.py:480
  68.8 2.9 %shard_map.79 = f32[32,256]{1,0:T(8,128)S(1)} custom-call(s32[256,128]{1,0:T(8,128)S(1)} %bitcast.19, f32[256,128]{1,0:T(8,128)S(1)} %bitcast.25), custom_call_target="tpu_custom_call" | custom-call | tf_op jit(solution)/shard_map/pallas_call | solution.py:91
  72.3 11.5 %all-to-all-start = ((f32[32,1,256]{2,1,0:T(1,128)}), f32[32,1,256]{2,1,0:T(1,128)}, u32[]{:S(2)}, u32[]{:S(2)}) async-start(f32[32,1,256]{2,1,0:T(1,128)} %copy.8), calls=%async_computation | async-start | bytes 65536 | tf_op jit(solution)/shard_map/all_to_all | solution.py:559
  83.9 8.0 %all-to-all-done = f32[32,1,256]{2,1,0:T(1,128)} async-done(((f32[32,1,256]{2,1,0:T(1,128)}), f32[32,1,256]{2,1,0:T(1,128)}, u32[]{:S(2)}, u32[]{:S(2)}) %all-to-all-start) | async-done | bytes 32800 | tf_op jit(solution)/shard_map/all_to_all | solution.py:559
  94.6 4.6 %all-to-all-start.1 = ((f32[32,1,128]{2,1,0:T(1,128)}), f32[32,1,128]{2,1,0:T(1,128)S(1)}, u32[]{:S(2)}, u32[]{:S(2)}) async-start(f32[32,1,128]{2,1,0:T(1,128)} %bitcast.30), calls=%async_computation.1 | async-start | bytes 32768 | tf_op jit(solution)/shard_map/all_to_all | solution.py:561
  99.3 1.0 constant_dynamic-slice_fusion.1
  100.3 2.5 %copy-done.4 = f32[10240,128]{1,0:T(8,128)S(1)} copy-done((f32[10240,128]{1,0:T(8,128)S(1)}, f32[10240,128]{1,0:T(8,128)}, u32[]{:S(2)}) %copy-start.4) | copy-done | bytes 5242904
  102.8 22.5 %shard_map.78.factor_ref = f32[32,384,128]{2,1,0:T(8,128)S(1)} custom-call(f32[32,320,128]{2,1,0:T(8,128)S(1)} %bitcast.18), custom_call_target="tpu_custom_call" | custom-call | tf_op jit(solution)/shard_map/pallas_call | solution.py:273
  125.3 2.7 %copy-done.2 = f32[32,384,128]{2,1,0:T(8,128)} copy-done((f32[32,384,128]{2,1,0:T(8,128)}, f32[32,384,128]{2,1,0:T(8,128)S(1)}, u32[]{:S(2)}) %copy-start.2) | copy-done | bytes 6291480
  128.0 2.6 %shard_map.77.unknown_ref = s32[256,128]{1,0:T(8,128)S(1)} custom-call(s32[256,128]{1,0:T(8,128)S(1)} %bitcast.20, f32[64,128]{1,0:T(8,128)S(1)} %pad_maximum_fusion.table_ref), custom_call_target="tpu_custom_call" | custom-call | tf_op jit(solution)/shard_map/pallas_call | solution.py:63
  131.2 2.8 %copy-done.3 = f32[32,384,128]{2,1,0:T(8,128)S(1)} copy-done((f32[32,384,128]{2,1,0:T(8,128)S(1)}, f32[32,384,128]{2,1,0:T(8,128)}, u32[]{:S(2)}) %copy-start.3) | copy-done | bytes 6291480
  134.1 4.6 %shard_map.81.table_ref = f32[32,128]{1,0:T(8,128)S(1)} custom-call(f32[32,384,128]{2,1,0:T(8,128)S(1)} %copy-done.3, f32[32,128]{1,0:T(8,128)S(1)} %bitcast.27), custom_call_target="tpu_custom_call" | custom-call | tf_op jit(solution)/shard_map/pallas_call | solution.py:312
  138.7 1.9 %shard_map.82.cells_ref = f32[8,32,128]{2,1,0:T(8,128)S(1)} custom-call(s32[256,128]{1,0:T(8,128)S(1)} %bitcast.21, s32[256,128]{1,0:T(8,128)S(1)} %copy-done.17, f32[32,128]{1,0:T(8,128)S(1)} %shard_map.81.table_ref, f32[8,32,128]{2,1,0:T(8,128)S(1)} %copy-done.25), custom_call_target="tpu_custom_call" | custom-call | tf_op jit(solution)/shard_map/pallas_call | solution.py:130
  140.6 4.3 %collective-permute-start.5 = (f32[3,32,128]{2,1,0:T(8,128)S(1)}, f32[3,32,128]{2,1,0:T(8,128)S(1)}, u32[]{:S(2)}, u32[]{:S(2)}) collective-permute-start(f32[3,32,128]{2,1,0:T(8,128)S(1)} %get-tuple-element.31), channel_id=1, source_target_pairs={{8,0},{16,8},{24,16},{32,24},{40,32},{48,40},{56,48},{64,56},{72,6... | collective-permute-start | bytes 147464 | tf_op jit(solution)/shard_map/ppermute | solution.py:525
  144.9 1.9 %collective-permute-start.4 = (f32[3,32,128]{2,1,0:T(8,128)S(1)}, f32[3,32,128]{2,1,0:T(8,128)S(1)}, u32[]{:S(2)}, u32[]{:S(2)}) collective-permute-start(f32[3,32,128]{2,1,0:T(8,128)S(1)} %get-tuple-element.32), channel_id=1, source_target_pairs={{0,8},{8,16},{16,24},{24,32},{32,40},{40,48},{48,56},{56,64},{64,7... | collective-permute-start | bytes 147464 | tf_op jit(solution)/shard_map/ppermute | solution.py:525
  146.9 5.0 %collective-permute-done.4.below_ref = f32[3,32,128]{2,1,0:T(8,128)S(1)} collective-permute-done((f32[3,32,128]{2,1,0:T(8,128)S(1)}, f32[3,32,128]{2,1,0:T(8,128)S(1)}, u32[]{:S(2)}, u32[]{:S(2)}) %collective-permute-start.4) | collective-permute-done | bytes 49184 | tf_op jit(solution)/shard_map/ppermute | solution.py:525
  151.9 11.3 %collective-permute-start.6 = (f32[14,3,128]{2,1,0:T(4,128)S(1)}, f32[14,3,128]{2,1,0:T(4,128)S(1)}, u32[]{:S(2)}, u32[]{:S(2)}) collective-permute-start(f32[14,3,128]{2,1,0:T(4,128)S(1)} %pad_maximum_fusion.1), channel_id=1, source_target_pairs={{0,1},{1,2},{2,3},{3,4},{4,5},{5,6},{6,7},{8,9},{9,10},{10,11},{11... | collective-permute-start | bytes 64520 | tf_op jit(solution)/shard_map/ppermute | solution.py:525
  163.2 1.9 %collective-permute-start.7 = (f32[14,3,128]{2,1,0:T(4,128)S(1)}, f32[14,3,128]{2,1,0:T(4,128)S(1)}, u32[]{:S(2)}, u32[]{:S(2)}) collective-permute-start(f32[14,3,128]{2,1,0:T(4,128)S(1)} %pad_maximum_fusion.2), channel_id=1, source_target_pairs={{1,0},{2,1},{3,2},{4,3},{5,4},{6,5},{7,6},{9,8},{10,9},{11,10},{12... | collective-permute-start | bytes 64520 | tf_op jit(solution)/shard_map/ppermute | solution.py:525
  165.2 3.3 %collective-permute-done.7.right_ref = f32[14,3,128]{2,1,0:T(4,128)S(1)} collective-permute-done((f32[14,3,128]{2,1,0:T(4,128)S(1)}, f32[14,3,128]{2,1,0:T(4,128)S(1)}, u32[]{:S(2)}, u32[]{:S(2)}) %collective-permute-start.7) | collective-permute-done | bytes 21536 | tf_op jit(solution)/shard_map/ppermute | solution.py:525
  168.4 4.9 %shard_map.83 = f32[8,32,128]{2,1,0:T(8,128)} custom-call(f32[6]{0:T(128)S(1)} %copy-done.30, f32[27,8,32,128]{3,2,1,0:T(8,128)S(1)} %copy-done.1, f32[224,8,128]{2,1,0:T(8,128)S(1)} %copy-done.10, f32[59,40,128]{2,1,0:T(8,128)S(1)} %copy-done.6, f32[59,40,128]{2,1,0:T(8,128)S(1)} %copy-done.8, f32[12,40,128]{2,1,0:T(8,128)S(1)} %copy-done.19, ...), custom_call_target="tpu_custom_call" | custom-call | tf_op jit(solution)/shard_map/pallas_call | solution.py:512
  (74 shorter events, 8.2 us)
Async XLA Ops:
  6.5 92.7 %all-gather.3.cloned.1.call-start = ((), (), s32[]{:S(2)}) async-start(), calls=%async_computation.2 | async-start | bytes 5406720 | tf_op jit(solution)/shard_map/all_gather | solution.py:548
  14.2 11.4 %copy-start.1 = (f32[27,8,32,128]{3,2,1,0:T(8,128)S(1)}, f32[27,8,32,128]{3,2,1,0:T(8,128)}, u32[]{:S(2)}) copy-start(f32[27,8,32,128]{3,2,1,0:T(8,128)} %main_ref.3) | copy-start | bytes 10616836
  14.2 11.4 %copy-start.12 = (f32[8,32,128]{2,1,0:T(8,128)S(1)}, f32[8,32,128]{2,1,0:T(8,128)}, u32[]{:S(2)}) copy-start(f32[8,32,128]{2,1,0:T(8,128)} %side_main_ref.1) | copy-start | bytes 393220
  14.2 48.7 %copy-start.29 = (f32[6]{0:T(128)S(1)}, f32[6]{0:T(128)}, u32[]{:S(2)}) copy-start(f32[6]{0:T(128)} %steps_ref.3) | copy-start | bytes 76
  14.4 6.8 %collective-permute-start = (f32[240,2,128]{2,1,0:T(2,128)S(1)}, f32[240,2,128]{2,1,0:T(2,128)S(1)}, u32[]{:S(2)}, u32[]{:S(2)}) collective-permute-start(f32[240,2,128]{2,1,0:T(2,128)S(1)} %get-tuple-element.17), channel_id=1, source_target_pairs={{0,1},{1,2},{2,3},{3,4},{4,5},{5,6},{6,7},{8,9},{9,10},{10,11},{11... | collective-permute-start | bytes 737288 | tf_op jit(solution)/shard_map/ppermute | solution.py:525
  18.1 7.5 %collective-permute-start.1 = (f32[240,2,128]{2,1,0:T(2,128)S(1)}, f32[240,2,128]{2,1,0:T(2,128)S(1)}, u32[]{:S(2)}, u32[]{:S(2)}) collective-permute-start(f32[240,2,128]{2,1,0:T(2,128)S(1)} %get-tuple-element.18), channel_id=1, source_target_pairs={{1,0},{2,1},{3,2},{4,3},{5,4},{6,5},{7,6},{9,8},{10,9},{11,10},{12... | collective-permute-start | bytes 737288 | tf_op jit(solution)/shard_map/ppermute | solution.py:525
  27.3 40.1 %copy-start.9 = (f32[224,8,128]{2,1,0:T(8,128)}, f32[224,8,128]{2,1,0:T(8,128)S(1)}, u32[]{:S(2)}) copy-start(f32[224,8,128]{2,1,0:T(8,128)S(1)} %get-tuple-element.19.edge_ref) | copy-start | bytes 2752516
  27.3 34.9 %collective-permute-start.2 = (f32[59,40,128]{2,1,0:T(8,128)S(1)}, f32[59,40,128]{2,1,0:T(8,128)S(1)}, u32[]{:S(2)}, u32[]{:S(2)}) collective-permute-start(f32[59,40,128]{2,1,0:T(8,128)S(1)} %get-tuple-element.20), channel_id=1, source_target_pairs={{0,8},{8,16},{16,24},{24,32},{32,40},{40,48},{48,56},{56,64},{64,7... | collective-permute-start | bytes 3624968 | tf_op jit(solution)/shard_map/ppermute | solution.py:525
  30.5 32.4 %collective-permute-start.3 = (f32[59,40,128]{2,1,0:T(8,128)S(1)}, f32[59,40,128]{2,1,0:T(8,128)S(1)}, u32[]{:S(2)}, u32[]{:S(2)}) collective-permute-start(f32[59,40,128]{2,1,0:T(8,128)S(1)} %get-tuple-element.21), channel_id=1, source_target_pairs={{8,0},{16,8},{24,16},{32,24},{40,32},{48,40},{56,48},{64,56},{72,6... | collective-permute-start | bytes 3624968 | tf_op jit(solution)/shard_map/ppermute | solution.py:525
  62.1 5.3 %copy-start.5 = (f32[59,40,128]{2,1,0:T(8,128)}, f32[59,40,128]{2,1,0:T(8,128)S(1)}, u32[]{:S(2)}) copy-start(f32[59,40,128]{2,1,0:T(8,128)S(1)} %collective-permute-done.2.low_ref) | copy-start | bytes 3624964
  62.9 4.5 %copy-start.7 = (f32[59,40,128]{2,1,0:T(8,128)}, f32[59,40,128]{2,1,0:T(8,128)S(1)}, u32[]{:S(2)}) copy-start(f32[59,40,128]{2,1,0:T(8,128)S(1)} %collective-permute-done.3.high_ref) | copy-start | bytes 3624964
  62.9 5.9 %copy-start.13 = (s32[8,32,128]{2,1,0:T(8,128)S(1)}, s32[8,32,128]{2,1,0:T(8,128)}, u32[]{:S(2)}) copy-start(s32[8,32,128]{2,1,0:T(8,128)} %param.10) | copy-start | bytes 393220
  68.8 2.9 %copy-start.18 = (f32[12,40,128]{2,1,0:T(8,128)}, f32[12,40,128]{2,1,0:T(8,128)S(1)}, u32[]{:S(2)}) copy-start(f32[12,40,128]{2,1,0:T(8,128)S(1)} %get-tuple-element.23.side_ref) | copy-start | bytes 737284
  72.3 19.5 %all-to-all-start = ((f32[32,1,256]{2,1,0:T(1,128)}), f32[32,1,256]{2,1,0:T(1,128)}, u32[]{:S(2)}, u32[]{:S(2)}) async-start(f32[32,1,256]{2,1,0:T(1,128)} %copy.8), calls=%async_computation | async-start | bytes 65536 | tf_op jit(solution)/shard_map/all_to_all | solution.py:559
  94.6 36.6 %all-to-all-start.1 = ((f32[32,1,128]{2,1,0:T(1,128)}), f32[32,1,128]{2,1,0:T(1,128)S(1)}, u32[]{:S(2)}, u32[]{:S(2)}) async-start(f32[32,1,128]{2,1,0:T(1,128)} %bitcast.30), calls=%async_computation.1 | async-start | bytes 32768 | tf_op jit(solution)/shard_map/all_to_all | solution.py:561
  100.3 2.5 %copy-start.4 = (f32[10240,128]{1,0:T(8,128)S(1)}, f32[10240,128]{1,0:T(8,128)}, u32[]{:S(2)}) copy-start(f32[10240,128]{1,0:T(8,128)} %all-gather.3.cloned.1.call-done) | copy-start | bytes 15728644
  102.8 25.2 %copy-start.14 = (s32[8,32,128]{2,1,0:T(8,128)S(1)}, s32[8,32,128]{2,1,0:T(8,128)}, u32[]{:S(2)}) copy-start(s32[8,32,128]{2,1,0:T(8,128)} %param.10) | copy-start | bytes 393220
  125.3 2.7 %copy-start.2 = (f32[32,384,128]{2,1,0:T(8,128)}, f32[32,384,128]{2,1,0:T(8,128)S(1)}, u32[]{:S(2)}) copy-start(f32[32,384,128]{2,1,0:T(8,128)S(1)} %shard_map.78.factor_ref) | copy-start | bytes 18874372
  131.2 2.8 %copy-start.3 = (f32[32,384,128]{2,1,0:T(8,128)S(1)}, f32[32,384,128]{2,1,0:T(8,128)}, u32[]{:S(2)}) copy-start(f32[32,384,128]{2,1,0:T(8,128)} %copy-done.2) | copy-start | bytes 18874372
  134.0 4.6 %copy-start.15 = (s32[8,32,128]{2,1,0:T(8,128)S(1)}, s32[8,32,128]{2,1,0:T(8,128)}, u32[]{:S(2)}) copy-start(s32[8,32,128]{2,1,0:T(8,128)} %param.10) | copy-start | bytes 393220
  134.0 4.6 %copy-start.17 = (s32[256,128]{1,0:T(8,128)S(1)}, s32[256,128]{1,0:T(8,128)}, u32[]{:S(2)}) copy-start(s32[256,128]{1,0:T(8,128)} %copy-done.16) | copy-start | bytes 393220
  134.0 4.6 %copy-start.25 = (f32[8,32,128]{2,1,0:T(8,128)S(1)}, f32[8,32,128]{2,1,0:T(8,128)}, u32[]{:S(2)}) copy-start(f32[8,32,128]{2,1,0:T(8,128)} %copy-done.24) | copy-start | bytes 393220
  134.0 34.4 %copy-start.6 = (f32[59,40,128]{2,1,0:T(8,128)S(1)}, f32[59,40,128]{2,1,0:T(8,128)}, u32[]{:S(2)}) copy-start(f32[59,40,128]{2,1,0:T(8,128)} %copy-done.5) | copy-start | bytes 3624964
  134.0 34.4 %copy-start.8 = (f32[59,40,128]{2,1,0:T(8,128)S(1)}, f32[59,40,128]{2,1,0:T(8,128)}, u32[]{:S(2)}) copy-start(f32[59,40,128]{2,1,0:T(8,128)} %copy-done.7) | copy-start | bytes 3624964
  134.1 34.4 %copy-start.10 = (f32[224,8,128]{2,1,0:T(8,128)S(1)}, f32[224,8,128]{2,1,0:T(8,128)}, u32[]{:S(2)}) copy-start(f32[224,8,128]{2,1,0:T(8,128)} %copy-done.9) | copy-start | bytes 2752516
  134.1 34.4 %copy-start.19 = (f32[12,40,128]{2,1,0:T(8,128)S(1)}, f32[12,40,128]{2,1,0:T(8,128)}, u32[]{:S(2)}) copy-start(f32[12,40,128]{2,1,0:T(8,128)} %copy-done.18) | copy-start | bytes 737284
  134.1 34.4 %copy-start.21 = (f32[12,40,128]{2,1,0:T(8,128)S(1)}, f32[12,40,128]{2,1,0:T(8,128)}, u32[]{:S(2)}) copy-start(f32[12,40,128]{2,1,0:T(8,128)} %copy-done.20) | copy-start | bytes 737284
  134.1 34.4 %copy-start.30 = (f32[6]{0:T(128)S(1)}, f32[6]{0:T(128)}, u32[]{:S(2)}) copy-start(f32[6]{0:T(128)} %steps_ref.3) | copy-start | bytes 76
  140.6 6.2 %collective-permute-start.5 = (f32[3,32,128]{2,1,0:T(8,128)S(1)}, f32[3,32,128]{2,1,0:T(8,128)S(1)}, u32[]{:S(2)}, u32[]{:S(2)}) collective-permute-start(f32[3,32,128]{2,1,0:T(8,128)S(1)} %get-tuple-element.31), channel_id=1, source_target_pairs={{8,0},{16,8},{24,16},{32,24},{40,32},{48,40},{56,48},{64,56},{72,6... | collective-permute-start | bytes 147464 | tf_op jit(solution)/shard_map/ppermute | solution.py:525
  144.9 6.9 %collective-permute-start.4 = (f32[3,32,128]{2,1,0:T(8,128)S(1)}, f32[3,32,128]{2,1,0:T(8,128)S(1)}, u32[]{:S(2)}, u32[]{:S(2)}) collective-permute-start(f32[3,32,128]{2,1,0:T(8,128)S(1)} %get-tuple-element.32), channel_id=1, source_target_pairs={{0,8},{8,16},{16,24},{24,32},{32,40},{40,48},{48,56},{56,64},{64,7... | collective-permute-start | bytes 147464 | tf_op jit(solution)/shard_map/ppermute | solution.py:525
  151.9 13.3 %collective-permute-start.6 = (f32[14,3,128]{2,1,0:T(4,128)S(1)}, f32[14,3,128]{2,1,0:T(4,128)S(1)}, u32[]{:S(2)}, u32[]{:S(2)}) collective-permute-start(f32[14,3,128]{2,1,0:T(4,128)S(1)} %pad_maximum_fusion.1), channel_id=1, source_target_pairs={{0,1},{1,2},{2,3},{3,4},{4,5},{5,6},{6,7},{8,9},{9,10},{10,11},{11... | collective-permute-start | bytes 64520 | tf_op jit(solution)/shard_map/ppermute | solution.py:525
  163.2 5.2 %collective-permute-start.7 = (f32[14,3,128]{2,1,0:T(4,128)S(1)}, f32[14,3,128]{2,1,0:T(4,128)S(1)}, u32[]{:S(2)}, u32[]{:S(2)}) collective-permute-start(f32[14,3,128]{2,1,0:T(4,128)S(1)} %pad_maximum_fusion.2), channel_id=1, source_target_pairs={{1,0},{2,1},{3,2},{4,3},{5,4},{6,5},{7,6},{9,8},{10,9},{11,10},{12... | collective-permute-start | bytes 64520 | tf_op jit(solution)/shard_map/ppermute | solution.py:525
  (10 other events, 8.8 us)
Sparse Core Ops, SparseCore 0:
  11.4 85.1 all-gather.2

commit v4 on v3

--- a/solution.py
+++ b/solution.py
@@ -48,7 +48,11 @@
     return ((slot >> 7) & 1) * 32 + (slot >> 8)
 
 
-def lookup_kernel(slot_ref, table_ref, out_ref):
+def lookup_kernel(place_ref, slot_ref, every_ref, out_ref, table_ref):
+    me = place_ref[0]
+    for owner in range(32):
+        table_ref[owner : owner + 1] = every_ref[owner, pl.ds(256 + me, 1)]
+        table_ref[32 + owner : 33 + owner] = every_ref[owner, pl.ds(288 + me, 1)]
     table = table_ref[...].astype(BF16)
 
     @pl.loop(0, slot_ref.shape[0] // 8, unroll=8)
@@ -59,12 +63,15 @@
         out_ref[where] = found.astype(jnp.int32)
 
 
-def lookup(slot, table):
+def lookup(place, slot, every):
+    vmem = pl.BlockSpec(memory_space=pltpu.VMEM)
     return pl.pallas_call(
         lookup_kernel,
         out_shape=jax.ShapeDtypeStruct(slot.shape, jnp.int32),
-        compiler_params=pltpu.CompilerParams(vmem_limit_bytes=8 * 2**20),
-    )(slot, table)
+        in_specs=[pl.BlockSpec(memory_space=pltpu.SMEM), vmem, vmem],
+        scratch_shapes=[pltpu.VMEM((64, 128), F32)],
+        compiler_params=pltpu.CompilerParams(vmem_limit_bytes=12 * 2**20),
+    )(place, slot, every)
 
 
 def scatter_kernel(slot_ref, value_ref, out_ref):
@@ -236,85 +243,76 @@
     )(place, diag, lower, index)
 
 
-def factor_kernel(count, every_ref, out_ref, d_ref, l_ref, x_ref, r_ref):
-    diag_ref = every_ref.at[:, 0:128]
-    lower_ref = every_ref.at[:, 128:256]
+def row3(form, row, mat):
+    rh, rl = split(row)
+    mh, ml = split(mat)
+    return form(rh, mh) + (form(rl, mh) + form(rh, ml))
+
+
+def chain_kernel(count, every_ref, rhs_ref, out_ref, kept_ref, d_ref, l_ref, x_ref, y_ref, r_ref):
     stride = 1
     while stride < count:
         gone = list(range(stride, count, 2 * stride))
-        src_d = diag_ref if stride == 1 else d_ref
-        src_l = lower_ref if stride == 1 else l_ref
+        src_d = every_ref.at[:, 0:128] if stride == 1 else d_ref
+        src_l = every_ref.at[:, 128:256] if stride == 1 else l_ref
         if stride > 1:
-            invert(len(gone), lambda b: src_d[gone[b]], x_ref, r_ref)
+            invert(len(gone), lambda b: src_d[gone[b]], x_ref, y_ref)
         for b, j in enumerate(gone):
-            inverse = diag_ref[j] if stride == 1 else x_ref[b]
-            out_ref[j, 0:128] = inverse
-            out_ref[j, 128:256] = mm3(nn, src_l[j].T, inverse)
+            inverse = src_d[j] if stride == 1 else x_ref[b]
+            kept_ref[j, 0:128] = inverse
+            kept_ref[j, 128:256] = mm3(nn, src_l[j].T, inverse)
             if j + stride < count:
-                out_ref[j, 256:384] = mm3(nn, src_l[j + stride], inverse)
-            else:
-                out_ref[j, 256:384] = jnp.zeros((128, 128), F32)
+                kept_ref[j, 256:384] = mm3(nn, src_l[j + stride], inverse)
         for i in range(0, count, 2 * stride):
             high = i + stride
-            value = src_d[i] - mm3(nn, out_ref[high, 128:256], src_l[high])
+            value = src_d[i] - mm3(nn, kept_ref[high, 128:256], src_l[high])
             if i > 0:
                 low = i - stride
-                qt = out_ref[low, 256:384]
-                value = value - mm3(nt, qt, src_l[i])
-                l_ref[i] = -mm3(nn, qt, src_l[low])
+                after = kept_ref[low, 256:384]
+                value = value - mm3(nt, after, src_l[i])
+                l_ref[i] = -mm3(nn, after, src_l[low])
             d_ref[i] = value
         stride *= 2
-    invert(1, lambda b: d_ref[0], x_ref, r_ref)
-    out_ref[0, 0:128] = x_ref[0]
-    out_ref[0, 128:384] = jnp.zeros((256, 128), F32)
-
-def factor(every):
+    invert(1, lambda b: d_ref[0], x_ref, y_ref)
+
+    r_ref[...] = rhs_ref[...]
+    stride = 1
+    while stride < count:
+        for j in range(stride, count, 2 * stride):
+            row = r_ref[pl.ds(j, 1)]
+            if j + stride < count:
+                t = row3(nt, row, kept_ref[j, 128:384])
+                r_ref[pl.ds(j + stride, 1)] = r_ref[pl.ds(j + stride, 1)] - t[:, 128:]
+            else:
+                t = row3(nt, row, kept_ref[j, 128:256])
+            r_ref[pl.ds(j - stride, 1)] = r_ref[pl.ds(j - stride, 1)] - t[:, :128]
+        stride *= 2
+    out_ref[0:1] = row3(nn, r_ref[0:1], x_ref[0])
+    while stride > 1:
+        stride //= 2
+        for j in range(stride, count, 2 * stride):
+            x = row3(nn, r_ref[pl.ds(j, 1)], kept_ref[j, 0:128])
+            x = x - row3(nn, out_ref[pl.ds(j - stride, 1)], kept_ref[j, 128:256])
+            if j + stride < count:
+                x = x - row3(nn, out_ref[pl.ds(j + stride, 1)], kept_ref[j, 256:384])
+            out_ref[pl.ds(j, 1)] = x
+
+
+def chain_solve(every, rhs):
     count = every.shape[0]
     return pl.pallas_call(
-        functools.partial(factor_kernel, count),
-        out_shape=jax.ShapeDtypeStruct((count, 384, 128), F32),
+        functools.partial(chain_kernel, count),
+        out_shape=jax.ShapeDtypeStruct((count, 128), F32),
         scratch_shapes=[
+            pltpu.VMEM((count, 384, 128), F32),
             pltpu.VMEM((count, 128, 128), F32),
             pltpu.VMEM((count, 128, 128), F32),
             pltpu.VMEM((count // 4, 128, 128), F32),
             pltpu.VMEM((count // 4, 128, 128), F32),
+            pltpu.VMEM((count, 128), F32),
         ],
-        compiler_params=pltpu.CompilerParams(vmem_limit_bytes=22 * 2**20),
-    )(every)
-
-
-def solve_kernel(count, factor_ref, rhs_ref, out_ref, r_ref):
-    def row3(form, row, mat):
-        rh, rl = split(row)
-        mh, ml = split(mat)
-        return form(rh, mh) + (form(rl, mh) + form(rh, ml))
-    r_ref[...] = rhs_ref[...]
-    stride = 1
-    while stride < count:
-        for j in range(stride, count, 2 * stride):
-            t = row3(nt, r_ref[pl.ds(j, 1)], factor_ref[j, 128:384])
-            r_ref[pl.ds(j - stride, 1)] = r_ref[pl.ds(j - stride, 1)] - t[:, :128]
-            if j + stride < count:
-                r_ref[pl.ds(j + stride, 1)] = r_ref[pl.ds(j + stride, 1)] - t[:, 128:]
-        stride *= 2
-    out_ref[0:1] = row3(nn, r_ref[0:1], factor_ref[0, 0:128])
-    while stride > 1:
-        stride //= 2
-        for j in range(stride, count, 2 * stride):
-            x = row3(nn, r_ref[pl.ds(j, 1)], factor_ref[j, 0:128])
-            x = x - row3(nn, out_ref[pl.ds(j - stride, 1)], factor_ref[j, 128:256])
-            if j + stride < count:
-                x = x - row3(nn, out_ref[pl.ds(j + stride, 1)], factor_ref[j, 256:384])
-            out_ref[pl.ds(j, 1)] = x
-
-def solve(factors, rhs):
-    count = rhs.shape[0]
-    return pl.pallas_call(
-        functools.partial(solve_kernel, count),
-        out_shape=jax.ShapeDtypeStruct((count, 128), F32),
-        scratch_shapes=[pltpu.VMEM((count, 128), F32)],
-        compiler_params=pltpu.CompilerParams(vmem_limit_bytes=10 * 2**20),
-    )(factors, rhs)
+        compiler_params=pltpu.CompilerParams(vmem_limit_bytes=24 * 2**20),
+    )(every, rhs)
 
 
 def cut_kernel(weights_ref, side_ref, next_ref, previous_ref, start_ref):
@@ -560,14 +558,8 @@
     mine_rhs = collect(index, arrived)
     rhs = lax.all_to_all(mine_rhs, "slab", split_axis=0, concat_axis=0, tiled=True)
 
-    table = jnp.concatenate(
-        [
-            lax.dynamic_index_in_dim(every, 256 + me, 1, False),
-            lax.dynamic_index_in_dim(every, 288 + me, 1, False),
-        ]
-    )
-    unknown = lookup(slot, table)
-    coarse_x = solve(factor(every), rhs)
+    unknown = lookup(place, slot, every)
+    coarse_x = chain_solve(every, rhs)
     corrected = gather(slot, unknown, coarse_x, smooth)
     return post_smooth(
         cheb_steps, stencil_weights, edge, low, high, side, inverse_center,

time: 181 us -> 174 us (0.961)
  the two profiles are of different devices: /device:TPU:33 before, /device:TPU:123 now
where the time goes in v4:
time: 174 us; the launch traced here: 171 us
  waiting for transfers between devices  49.8 us (29%)
  Pallas kernels  48.6 us (28%)
  starting transfers between devices  33.5 us (19%)
  between operations  13.8 us (8%)
  local copies, waits for them, and re-layouts  13.3 us (8%)
  blocking collectives  11.5 us (7%)
    ppermute x4, waiting for transfers between devices, from_sides(): lax.ppermute(to_next, axis, forward)  30.9 us
    pallas_call x1, Pallas kernels, chain_solve(): pl.pallas_call(functools.partial(chain_kernel, count), out_shape=jax.Shap...  26.9 us
    ppermute x4, waiting for transfers between devices, from_sides(): lax.ppermute(to_previous, axis, backward)  18.9 us
    ppermute x4, starting transfers between devices, from_sides(): lax.ppermute(to_next, axis, forward)  14.3 us
    unnamed x61, local copies, waits for them, and re-layouts  13.3 us
    all_to_all x1, blocking collectives, shards(): lax.all_to_all(sums, 'slab', split_axis=0, concat_axis=0, tiled=True)  11.5 us
    ppermute x4, starting transfers between devices, from_sides(): lax.ppermute(to_previous, axis, backward)  11.5 us
    all_to_all x1, starting transfers between devices, shards(): lax.all_to_all(mine_rhs, 'slab', split_axis=0, concat_axis=0, tiled=True)  7.69 us
  transfers between devices with their start and end apart: 10, of which 6 were waited for; matrix products, arithmetic and copies ran while one was open for 0% of the time, Pallas kernels for 7%

profile of v4, /device:TPU:123, one launch (start us, length us, event | category | flops | bytes accessed | tf_op | source)
XLA Modules:
  0.0 170.5 jit_solution(15963827457984452323)
XLA Ops:
  6.5 0.8 copy-done.21
  7.3 0.8 copy-done.25
  8.1 0.8 copy-done.26
  9.0 2.3 %shard_map.76 = f32[320,128]{1,0:T(8,128)} custom-call(s32[1]{0:T(128)} %bitcast.1.place_ref, f32[128,128]{1,0:T(8,128)S(1)} %bitcast.26, f32[128,128]{1,0:T(8,128)S(1)} %bitcast.27, s32[32,256]{1,0:T(8,128)S(1)} %bitcast.20), custom_call_target="tpu_custom_call" | custom-call | tf_op jit(solution)/shard_map/pallas_call | solution.py:237
  11.3 2.0 %copy-done = f32[27,8,32,128]{3,2,1,0:T(8,128)S(1)} copy-done((f32[27,8,32,128]{3,2,1,0:T(8,128)S(1)}, f32[27,8,32,128]{3,2,1,0:T(8,128)}, u32[]{:S(2)}) %copy-start) | copy-done | bytes 3538968
  13.3 0.9 copy-done.10
  14.4 3.9 %collective-permute-start = (f32[240,2,128]{2,1,0:T(2,128)S(1)}, f32[240,2,128]{2,1,0:T(2,128)S(1)}, u32[]{:S(2)}, u32[]{:S(2)}) collective-permute-start(f32[240,2,128]{2,1,0:T(2,128)S(1)} %get-tuple-element.17), channel_id=1, source_target_pairs={{0,1},{1,2},{2,3},{3,4},{4,5},{5,6},{6,7},{8,9},{9,10},{10,11},{11... | collective-permute-start | bytes 737288 | tf_op jit(solution)/shard_map/ppermute | solution.py:523
  18.3 1.9 %collective-permute-start.1 = (f32[240,2,128]{2,1,0:T(2,128)S(1)}, f32[240,2,128]{2,1,0:T(2,128)S(1)}, u32[]{:S(2)}, u32[]{:S(2)}) collective-permute-start(f32[240,2,128]{2,1,0:T(2,128)S(1)} %get-tuple-element.18), channel_id=1, source_target_pairs={{1,0},{2,1},{3,2},{4,3},{5,4},{6,5},{7,6},{9,8},{10,9},{11,10},{12... | collective-permute-start | bytes 737288 | tf_op jit(solution)/shard_map/ppermute | solution.py:523
  20.2 1.2 collective-permute-done.left_ref
  21.4 4.4 %collective-permute-done.1.right_ref = f32[240,2,128]{2,1,0:T(2,128)S(1)} collective-permute-done((f32[240,2,128]{2,1,0:T(2,128)S(1)}, f32[240,2,128]{2,1,0:T(2,128)S(1)}, u32[]{:S(2)}, u32[]{:S(2)}) %collective-permute-start.1) | collective-permute-done | bytes 245792 | tf_op jit(solution)/shard_map/ppermute | solution.py:523
  25.8 1.7 shard_map.74
  27.5 4.1 %collective-permute-start.2 = (f32[59,40,128]{2,1,0:T(8,128)S(1)}, f32[59,40,128]{2,1,0:T(8,128)S(1)}, u32[]{:S(2)}, u32[]{:S(2)}) collective-permute-start(f32[59,40,128]{2,1,0:T(8,128)S(1)} %get-tuple-element.20), channel_id=1, source_target_pairs={{0,8},{8,16},{16,24},{24,32},{32,40},{40,48},{48,56},{56,64},{64,7... | collective-permute-start | bytes 3624968 | tf_op jit(solution)/shard_map/ppermute | solution.py:523
  31.7 1.9 %collective-permute-start.3 = (f32[59,40,128]{2,1,0:T(8,128)S(1)}, f32[59,40,128]{2,1,0:T(8,128)S(1)}, u32[]{:S(2)}, u32[]{:S(2)}) collective-permute-start(f32[59,40,128]{2,1,0:T(8,128)S(1)} %get-tuple-element.21), channel_id=1, source_target_pairs={{8,0},{16,8},{24,16},{32,24},{40,32},{48,40},{56,48},{64,56},{72,6... | collective-permute-start | bytes 3624968 | tf_op jit(solution)/shard_map/ppermute | solution.py:523
  33.6 28.6 %collective-permute-done.2.low_ref = f32[59,40,128]{2,1,0:T(8,128)S(1)} collective-permute-done((f32[59,40,128]{2,1,0:T(8,128)S(1)}, f32[59,40,128]{2,1,0:T(8,128)S(1)}, u32[]{:S(2)}, u32[]{:S(2)}) %collective-permute-start.2) | collective-permute-done | bytes 1208352 | tf_op jit(solution)/shard_map/ppermute | solution.py:523
  62.2 8.3 %collective-permute-done.3.high_ref = f32[59,40,128]{2,1,0:T(8,128)S(1)} collective-permute-done((f32[59,40,128]{2,1,0:T(8,128)S(1)}, f32[59,40,128]{2,1,0:T(8,128)S(1)}, u32[]{:S(2)}, u32[]{:S(2)}) %collective-permute-start.3) | collective-permute-done | bytes 1208352 | tf_op jit(solution)/shard_map/ppermute | solution.py:523
  70.5 4.5 %shard_map.75 = (f32[8,32,128]{2,1,0:T(8,128)S(1)}, f32[8,32,128]{2,1,0:T(8,128)S(1)}, f32[12,40,128]{2,1,0:T(8,128)S(1)}, f32[12,40,128]{2,1,0:T(8,128)S(1)}) custom-call(f32[6]{0:T(128)S(1)} %copy-done.28, f32[27,8,32,128]{3,2,1,0:T(8,128)S(1)} %copy-done.1, f32[224,8,128]{2,1,0:T(8,128)S(1)} %get-tuple-element.19.edge_ref, ...), custom_call_target="tpu_custom_call" | custom-call | tf_op jit(solution)/shard_map/pallas_call | solution.py:478
  75.7 2.9 %shard_map.78 = f32[32,256]{1,0:T(8,128)S(1)} custom-call(s32[256,128]{1,0:T(8,128)S(1)} %bitcast.17, f32[256,128]{1,0:T(8,128)S(1)} %bitcast.23), custom_call_target="tpu_custom_call" | custom-call | tf_op jit(solution)/shard_map/pallas_call | solution.py:98
  78.7 11.5 %all_to_all.22 = f32[32,1,256]{2,1,0:T(1,128)S(1)} all-to-all(f32[32,1,256]{2,1,0:T(1,128)S(1)} %copy.8), channel_id=1, replica_groups=mesh['slab'=32,'col'=8] {'slab'}, dimensions={0} | all-to-all | bytes 65536 | tf_op jit(solution)/shard_map/all_to_all | solution.py:557
  91.5 7.7 %all-to-all-start.1 = ((f32[32,1,128]{2,1,0:T(1,128)}), f32[32,1,128]{2,1,0:T(1,128)S(1)}, u32[]{:S(2)}, u32[]{:S(2)}) async-start(f32[32,1,128]{2,1,0:T(1,128)} %bitcast.28), calls=%async_computation.1 | async-start | bytes 32768 | tf_op jit(solution)/shard_map/all_to_all | solution.py:559
  99.2 2.5 %copy-done.2 = f32[10240,128]{1,0:T(8,128)S(1)} copy-done((f32[10240,128]{1,0:T(8,128)S(1)}, f32[10240,128]{1,0:T(8,128)}, u32[]{:S(2)}) %copy-start.2) | copy-done | bytes 5242904
  101.7 0.9 copy-done.13
  102.6 2.6 %shard_map.77.unknown_ref = s32[256,128]{1,0:T(8,128)S(1)} custom-call(s32[1]{0:T(128)} %bitcast.1.place_ref, s32[256,128]{1,0:T(8,128)S(1)} %bitcast.18, f32[32,320,128]{2,1,0:T(8,128)S(1)} %bitcast.15), custom_call_target="tpu_custom_call" | custom-call | tf_op jit(solution)/shard_map/pallas_call | solution.py:68
  105.8 2.5 %copy-done.3 = f32[10240,128]{1,0:T(8,128)S(1)} copy-done((f32[10240,128]{1,0:T(8,128)S(1)}, f32[10240,128]{1,0:T(8,128)}, u32[]{:S(2)}) %copy-start.3) | copy-done | bytes 5242904
  108.4 26.9 %shard_map.80.table_ref = f32[32,128]{1,0:T(8,128)S(1)} custom-call(f32[32,320,128]{2,1,0:T(8,128)S(1)} %bitcast.16, f32[32,128]{1,0:T(8,128)S(1)} %bitcast.25), custom_call_target="tpu_custom_call" | custom-call | tf_op jit(solution)/shard_map/pallas_call | solution.py:303
  135.4 1.9 %shard_map.81.cells_ref = f32[8,32,128]{2,1,0:T(8,128)S(1)} custom-call(s32[256,128]{1,0:T(8,128)S(1)} %bitcast.19, s32[256,128]{1,0:T(8,128)S(1)} %copy-done.16, f32[32,128]{1,0:T(8,128)S(1)} %shard_map.80.table_ref, f32[8,32,128]{2,1,0:T(8,128)S(1)} %copy-done.24), custom_call_target="tpu_custom_call" | custom-call | tf_op jit(solution)/shard_map/pallas_call | solution.py:137
  137.3 4.3 %collective-permute-start.4 = (f32[3,32,128]{2,1,0:T(8,128)S(1)}, f32[3,32,128]{2,1,0:T(8,128)S(1)}, u32[]{:S(2)}, u32[]{:S(2)}) collective-permute-start(f32[3,32,128]{2,1,0:T(8,128)S(1)} %get-tuple-element.30), channel_id=1, source_target_pairs={{0,8},{8,16},{16,24},{24,32},{32,40},{40,48},{48,56},{56,64},{64,7... | collective-permute-start | bytes 147464 | tf_op jit(solution)/shard_map/ppermute | solution.py:523
  141.6 1.9 %collective-permute-start.5 = (f32[3,32,128]{2,1,0:T(8,128)S(1)}, f32[3,32,128]{2,1,0:T(8,128)S(1)}, u32[]{:S(2)}, u32[]{:S(2)}) collective-permute-start(f32[3,32,128]{2,1,0:T(8,128)S(1)} %get-tuple-element.29), channel_id=1, source_target_pairs={{8,0},{16,8},{24,16},{32,24},{40,32},{48,40},{56,48},{64,56},{72,6... | collective-permute-start | bytes 147464 | tf_op jit(solution)/shard_map/ppermute | solution.py:523
  143.6 6.2 %collective-permute-done.5.beyond_ref = f32[3,32,128]{2,1,0:T(8,128)S(1)} collective-permute-done((f32[3,32,128]{2,1,0:T(8,128)S(1)}, f32[3,32,128]{2,1,0:T(8,128)S(1)}, u32[]{:S(2)}, u32[]{:S(2)}) %collective-permute-start.5) | collective-permute-done | bytes 49184 | tf_op jit(solution)/shard_map/ppermute | solution.py:523
  149.8 5.7 %collective-permute-start.7 = (f32[14,3,128]{2,1,0:T(4,128)S(1)}, f32[14,3,128]{2,1,0:T(4,128)S(1)}, u32[]{:S(2)}, u32[]{:S(2)}) collective-permute-start(f32[14,3,128]{2,1,0:T(4,128)S(1)} %pad_maximum_fusion.1), channel_id=1, source_target_pairs={{1,0},{2,1},{3,2},{4,3},{5,4},{6,5},{7,6},{9,8},{10,9},{11,10},{12... | collective-permute-start | bytes 64520 | tf_op jit(solution)/shard_map/ppermute | solution.py:523
  155.5 1.9 %collective-permute-start.6 = (f32[14,3,128]{2,1,0:T(4,128)S(1)}, f32[14,3,128]{2,1,0:T(4,128)S(1)}, u32[]{:S(2)}, u32[]{:S(2)}) collective-permute-start(f32[14,3,128]{2,1,0:T(4,128)S(1)} %pad_maximum_fusion), channel_id=1, source_target_pairs={{0,1},{1,2},{2,3},{3,4},{4,5},{5,6},{6,7},{8,9},{9,10},{10,11},{11... | collective-permute-start | bytes 64520 | tf_op jit(solution)/shard_map/ppermute | solution.py:523
  157.5 1.2 collective-permute-done.6.left_ref
  158.7 5.0 %shard_map.82 = f32[8,32,128]{2,1,0:T(8,128)} custom-call(f32[6]{0:T(128)S(1)} %copy-done.29, f32[27,8,32,128]{3,2,1,0:T(8,128)S(1)} %copy-done.1, f32[224,8,128]{2,1,0:T(8,128)S(1)} %copy-done.9, f32[59,40,128]{2,1,0:T(8,128)S(1)} %copy-done.5, f32[59,40,128]{2,1,0:T(8,128)S(1)} %copy-done.7, f32[12,40,128]{2,1,0:T(8,128)S(1)} %copy-done.18, ...), custom_call_target="tpu_custom_call" | custom-call | tf_op jit(solution)/shard_map/pallas_call | solution.py:510
  (68 shorter events, 3.0 us)
Async XLA Ops:
  6.5 92.6 %all-gather.3.cloned.1.call-start = ((), (), s32[]{:S(2)}) async-start(), calls=%async_computation.2 | async-start | bytes 5406720 | tf_op jit(solution)/shard_map/all_gather | solution.py:546
  11.3 2.0 %copy-start = (f32[27,8,32,128]{3,2,1,0:T(8,128)S(1)}, f32[27,8,32,128]{3,2,1,0:T(8,128)}, u32[]{:S(2)}) copy-start(f32[27,8,32,128]{3,2,1,0:T(8,128)} %main_ref.3) | copy-start | bytes 10616836
  14.2 11.7 %copy-start.1 = (f32[27,8,32,128]{3,2,1,0:T(8,128)S(1)}, f32[27,8,32,128]{3,2,1,0:T(8,128)}, u32[]{:S(2)}) copy-start(f32[27,8,32,128]{3,2,1,0:T(8,128)} %main_ref.3) | copy-start | bytes 10616836
  14.2 11.7 %copy-start.11 = (f32[8,32,128]{2,1,0:T(8,128)S(1)}, f32[8,32,128]{2,1,0:T(8,128)}, u32[]{:S(2)}) copy-start(f32[8,32,128]{2,1,0:T(8,128)} %side_main_ref.1) | copy-start | bytes 393220
  14.4 7.1 %collective-permute-start = (f32[240,2,128]{2,1,0:T(2,128)S(1)}, f32[240,2,128]{2,1,0:T(2,128)S(1)}, u32[]{:S(2)}, u32[]{:S(2)}) collective-permute-start(f32[240,2,128]{2,1,0:T(2,128)S(1)} %get-tuple-element.17), channel_id=1, source_target_pairs={{0,1},{1,2},{2,3},{3,4},{4,5},{5,6},{6,7},{8,9},{9,10},{10,11},{11... | collective-permute-start | bytes 737288 | tf_op jit(solution)/shard_map/ppermute | solution.py:523
  18.3 7.5 %collective-permute-start.1 = (f32[240,2,128]{2,1,0:T(2,128)S(1)}, f32[240,2,128]{2,1,0:T(2,128)S(1)}, u32[]{:S(2)}, u32[]{:S(2)}) collective-permute-start(f32[240,2,128]{2,1,0:T(2,128)S(1)} %get-tuple-element.18), channel_id=1, source_target_pairs={{1,0},{2,1},{3,2},{4,3},{5,4},{6,5},{7,6},{9,8},{10,9},{11,10},{12... | collective-permute-start | bytes 737288 | tf_op jit(solution)/shard_map/ppermute | solution.py:523
  25.8 44.6 %copy-start.28 = (f32[6]{0:T(128)S(1)}, f32[6]{0:T(128)}, u32[]{:S(2)}) copy-start(f32[6]{0:T(128)} %steps_ref.3) | copy-start | bytes 76
  27.5 47.4 %copy-start.8 = (f32[224,8,128]{2,1,0:T(8,128)}, f32[224,8,128]{2,1,0:T(8,128)S(1)}, u32[]{:S(2)}) copy-start(f32[224,8,128]{2,1,0:T(8,128)S(1)} %get-tuple-element.19.edge_ref) | copy-start | bytes 2752516
  27.5 34.6 %collective-permute-start.2 = (f32[59,40,128]{2,1,0:T(8,128)S(1)}, f32[59,40,128]{2,1,0:T(8,128)S(1)}, u32[]{:S(2)}, u32[]{:S(2)}) collective-permute-start(f32[59,40,128]{2,1,0:T(8,128)S(1)} %get-tuple-element.20), channel_id=1, source_target_pairs={{0,8},{8,16},{16,24},{24,32},{32,40},{40,48},{48,56},{56,64},{64,7... | collective-permute-start | bytes 3624968 | tf_op jit(solution)/shard_map/ppermute | solution.py:523
  31.7 38.8 %collective-permute-start.3 = (f32[59,40,128]{2,1,0:T(8,128)S(1)}, f32[59,40,128]{2,1,0:T(8,128)S(1)}, u32[]{:S(2)}, u32[]{:S(2)}) collective-permute-start(f32[59,40,128]{2,1,0:T(8,128)S(1)} %get-tuple-element.21), channel_id=1, source_target_pairs={{8,0},{16,8},{24,16},{32,24},{40,32},{48,40},{56,48},{64,56},{72,6... | collective-permute-start | bytes 3624968 | tf_op jit(solution)/shard_map/ppermute | solution.py:523
  62.2 12.8 %copy-start.4 = (f32[59,40,128]{2,1,0:T(8,128)}, f32[59,40,128]{2,1,0:T(8,128)S(1)}, u32[]{:S(2)}) copy-start(f32[59,40,128]{2,1,0:T(8,128)S(1)} %collective-permute-done.2.low_ref) | copy-start | bytes 3624964
  70.5 4.5 %copy-start.6 = (f32[59,40,128]{2,1,0:T(8,128)}, f32[59,40,128]{2,1,0:T(8,128)S(1)}, u32[]{:S(2)}) copy-start(f32[59,40,128]{2,1,0:T(8,128)S(1)} %collective-permute-done.3.high_ref) | copy-start | bytes 3624964
  70.5 5.3 %copy-start.12 = (s32[8,32,128]{2,1,0:T(8,128)S(1)}, s32[8,32,128]{2,1,0:T(8,128)}, u32[]{:S(2)}) copy-start(s32[8,32,128]{2,1,0:T(8,128)} %param.10) | copy-start | bytes 393220
  70.5 19.7 %copy-start.22 = (s32[1,1,32,256]{3,2,1,0:T(8,128)S(1)}, s32[1,1,32,256]{3,2,1,0:T(8,128)}, u32[]{:S(2)}) copy-start(s32[1,1,32,256]{3,2,1,0:T(8,128)} %param.11) | copy-start | bytes 98308
  75.7 2.9 %copy-start.17 = (f32[12,40,128]{2,1,0:T(8,128)}, f32[12,40,128]{2,1,0:T(8,128)S(1)}, u32[]{:S(2)}) copy-start(f32[12,40,128]{2,1,0:T(8,128)S(1)} %get-tuple-element.23.side_ref) | copy-start | bytes 737284
  75.7 15.1 %copy-start.23 = (f32[8,32,128]{2,1,0:T(8,128)}, f32[8,32,128]{2,1,0:T(8,128)S(1)}, u32[]{:S(2)}) copy-start(f32[8,32,128]{2,1,0:T(8,128)S(1)} %get-tuple-element.26.base_ref) | copy-start | bytes 393220
  91.5 14.4 %all-to-all-start.1 = ((f32[32,1,128]{2,1,0:T(1,128)}), f32[32,1,128]{2,1,0:T(1,128)S(1)}, u32[]{:S(2)}, u32[]{:S(2)}) async-start(f32[32,1,128]{2,1,0:T(1,128)} %bitcast.28), calls=%async_computation.1 | async-start | bytes 32768 | tf_op jit(solution)/shard_map/all_to_all | solution.py:559
  99.2 2.5 %copy-start.2 = (f32[10240,128]{1,0:T(8,128)S(1)}, f32[10240,128]{1,0:T(8,128)}, u32[]{:S(2)}) copy-start(f32[10240,128]{1,0:T(8,128)} %all-gather.3.cloned.1.call-done) | copy-start | bytes 15728644
  105.8 2.5 %copy-start.3 = (f32[10240,128]{1,0:T(8,128)S(1)}, f32[10240,128]{1,0:T(8,128)}, u32[]{:S(2)}) copy-start(f32[10240,128]{1,0:T(8,128)} %all-gather.3.cloned.1.call-done) | copy-start | bytes 15728644
  108.3 27.0 %copy-start.14 = (s32[8,32,128]{2,1,0:T(8,128)S(1)}, s32[8,32,128]{2,1,0:T(8,128)}, u32[]{:S(2)}) copy-start(s32[8,32,128]{2,1,0:T(8,128)} %param.10) | copy-start | bytes 393220
  108.3 27.0 %copy-start.16 = (s32[256,128]{1,0:T(8,128)S(1)}, s32[256,128]{1,0:T(8,128)}, u32[]{:S(2)}) copy-start(s32[256,128]{1,0:T(8,128)} %copy-done.15) | copy-start | bytes 393220
  108.3 27.0 %copy-start.24 = (f32[8,32,128]{2,1,0:T(8,128)S(1)}, f32[8,32,128]{2,1,0:T(8,128)}, u32[]{:S(2)}) copy-start(f32[8,32,128]{2,1,0:T(8,128)} %copy-done.23) | copy-start | bytes 393220
  108.3 50.3 %copy-start.5 = (f32[59,40,128]{2,1,0:T(8,128)S(1)}, f32[59,40,128]{2,1,0:T(8,128)}, u32[]{:S(2)}) copy-start(f32[59,40,128]{2,1,0:T(8,128)} %copy-done.4) | copy-start | bytes 3624964
  108.3 50.3 %copy-start.7 = (f32[59,40,128]{2,1,0:T(8,128)S(1)}, f32[59,40,128]{2,1,0:T(8,128)}, u32[]{:S(2)}) copy-start(f32[59,40,128]{2,1,0:T(8,128)} %copy-done.6) | copy-start | bytes 3624964
  108.3 50.3 %copy-start.18 = (f32[12,40,128]{2,1,0:T(8,128)S(1)}, f32[12,40,128]{2,1,0:T(8,128)}, u32[]{:S(2)}) copy-start(f32[12,40,128]{2,1,0:T(8,128)} %copy-done.17) | copy-start | bytes 737284
  108.4 50.3 %copy-start.20 = (f32[12,40,128]{2,1,0:T(8,128)S(1)}, f32[12,40,128]{2,1,0:T(8,128)}, u32[]{:S(2)}) copy-start(f32[12,40,128]{2,1,0:T(8,128)} %copy-done.19) | copy-start | bytes 737284
  108.4 50.3 %copy-start.29 = (f32[6]{0:T(128)S(1)}, f32[6]{0:T(128)}, u32[]{:S(2)}) copy-start(f32[6]{0:T(128)} %steps_ref.3) | copy-start | bytes 76
  135.3 23.3 %copy-start.9 = (f32[224,8,128]{2,1,0:T(8,128)S(1)}, f32[224,8,128]{2,1,0:T(8,128)}, u32[]{:S(2)}) copy-start(f32[224,8,128]{2,1,0:T(8,128)} %copy-done.8) | copy-start | bytes 2752516
  137.3 6.3 %collective-permute-start.4 = (f32[3,32,128]{2,1,0:T(8,128)S(1)}, f32[3,32,128]{2,1,0:T(8,128)S(1)}, u32[]{:S(2)}, u32[]{:S(2)}) collective-permute-start(f32[3,32,128]{2,1,0:T(8,128)S(1)} %get-tuple-element.30), channel_id=1, source_target_pairs={{0,8},{8,16},{16,24},{24,32},{32,40},{40,48},{48,56},{56,64},{64,7... | collective-permute-start | bytes 147464 | tf_op jit(solution)/shard_map/ppermute | solution.py:523
  141.6 8.2 %collective-permute-start.5 = (f32[3,32,128]{2,1,0:T(8,128)S(1)}, f32[3,32,128]{2,1,0:T(8,128)S(1)}, u32[]{:S(2)}, u32[]{:S(2)}) collective-permute-start(f32[3,32,128]{2,1,0:T(8,128)S(1)} %get-tuple-element.29), channel_id=1, source_target_pairs={{8,0},{16,8},{24,16},{32,24},{40,32},{48,40},{56,48},{64,56},{72,6... | collective-permute-start | bytes 147464 | tf_op jit(solution)/shard_map/ppermute | solution.py:523
  149.8 7.7 %collective-permute-start.7 = (f32[14,3,128]{2,1,0:T(4,128)S(1)}, f32[14,3,128]{2,1,0:T(4,128)S(1)}, u32[]{:S(2)}, u32[]{:S(2)}) collective-permute-start(f32[14,3,128]{2,1,0:T(4,128)S(1)} %pad_maximum_fusion.1), channel_id=1, source_target_pairs={{1,0},{2,1},{3,2},{4,3},{5,4},{6,5},{7,6},{9,8},{10,9},{11,10},{12... | collective-permute-start | bytes 64520 | tf_op jit(solution)/shard_map/ppermute | solution.py:523
  155.5 3.1 %collective-permute-start.6 = (f32[14,3,128]{2,1,0:T(4,128)S(1)}, f32[14,3,128]{2,1,0:T(4,128)S(1)}, u32[]{:S(2)}, u32[]{:S(2)}) collective-permute-start(f32[14,3,128]{2,1,0:T(4,128)S(1)} %pad_maximum_fusion), channel_id=1, source_target_pairs={{0,1},{1,2},{2,3},{3,4},{4,5},{5,6},{6,7},{8,9},{9,10},{10,11},{11... | collective-permute-start | bytes 64520 | tf_op jit(solution)/shard_map/ppermute | solution.py:523
  (8 other events, 6.2 us)
Sparse Core Ops, SparseCore 0:
  11.4 85.2 all-gather.2
